TPU v7x, 512 devices: a whole 4x4x16 slice. The times are simulated.
512 devices in a mesh: dp: 16 (over z), expert: 32 (over x, y, core).
Axes of the slice: x: 4, y: 4, z: 16, core: 2. Of those that a mesh axis runs over, the one named last changes fastest.
Arguments:
- tokens: bfloat16 [1792, 4096], P('expert', 'dp'), may hold values from -6 to 6
- route_ids: int32 [1792, 8], P('expert'), may hold values from 0 to 63, as said below
- route_weights: float32 [1792, 8], P('expert'), may hold values from 0.05 to 0.5
- w_gate: bfloat16 [64, 4096, 768], P('expert', 'dp'), may hold values from -0.09375 to 0.09375
- w_up: bfloat16 [64, 4096, 768], P('expert', 'dp'), may hold values from -0.09375 to 0.09375
- w_down: bfloat16 [64, 768, 4096], P('expert', None, 'dp'), may hold values from -0.21875 to 0.21875
Outputs:
- moe_out: bfloat16 [1792, 4096], P('expert', 'dp')
- expert_loads: int32 [64], P('expert')
Inputs may be any that keep to these rules, and one draw needn't show every extreme that they name: `route_ids`: A token's 8 experts differ. Among the 56 tokens of one group no expert is chosen by more than 21 of them, and in every group some expert is chosen by exactly 21.
All inputs are finite; a program needn't handle non-finite values.
Results may differ from a plain program's by a relative error of at most 0.035.
Values may be sent and summed in bfloat16 or wider, within the bound.
No kernel may reach another device: no remote copies, remote signals or barrier semaphores. Data moves between devices by JAX's collectives and lax.ppermute only.
A program may use at most 64 MiB of HBM per device.

v0:
```python
import functools

import jax
import jax.numpy as jnp
from jax import lax
from jax.experimental import pallas as pl
from jax.experimental.pallas import tpu as pltpu
from jax.sharding import PartitionSpec as P

BF = jnp.bfloat16
F32 = jnp.float32
PIECE = 16
ROWS = 576
CHUNK = 192
NT = (((1,), (1,)), ((), ()))
PARAMS = pltpu.CompilerParams(vmem_limit_bytes=48 * 1024 * 1024)


def dot(a, b):
    return jnp.dot(a, b, preferred_element_type=F32)


def dot_nt(a, b):
    return lax.dot_general(a, b, NT, preferred_element_type=F32)


def iota(shape, dim):
    return lax.broadcasted_iota(jnp.int32, shape, dim)


def floor_div(value, by, limit):
    shift = 1
    while (1 << shift) < limit * by:
        shift += 1
    return (value * (-(-(1 << shift) // by))) >> shift


class Layout:
    def __init__(self, columns, capacity, exp_dev):
        self.columns, self.capacity, self.exp_dev = columns, capacity, exp_dev
        self.slots = capacity * exp_dev
        self.rows = -(-(self.slots + 1) // 16) * 16
        self.total = columns * self.rows
        self.experts = columns * exp_dev

    def split(self, row):
        block = floor_div(row, self.rows, self.total)
        place = row - block * self.rows
        within = jnp.zeros_like(place)
        for other in range(1, self.exp_dev):
            within = within + (place >= other * self.capacity).astype(jnp.int32)
        return block, place, within, place - within * self.capacity


def positions(ids_ref, lay):
    tokens, top_k = ids_ref.shape
    ids = ids_ref[...]
    lanes = iota((tokens, lay.experts), 1)
    chose = jnp.zeros((tokens, lay.experts), F32)
    for s in range(top_k):
        chose = chose + (ids[:, s : s + 1] == lanes).astype(F32)
    before = (iota((tokens, tokens), 0) > iota((tokens, tokens), 1)).astype(F32).astype(BF)
    rank = dot(before, chose.astype(BF))
    return chose, jnp.where(chose > 0, rank, -1.0)


def dispatch_kernel(lay, ids_ref, tokens_ref, out_ref):
    tokens, width = tokens_ref.shape
    padded = -(-tokens // 8) * 8 + 8
    chose, slot = positions(ids_ref, lay)
    ones = jnp.ones((8, tokens), BF)
    counts = dot(ones, chose.astype(BF))
    counts = jnp.concatenate([counts, jnp.zeros((8, width - lay.experts), F32)], axis=1)
    extended = [tokens_ref[...].astype(F32), counts]
    if padded - 8 > tokens:
        extended.insert(1, jnp.zeros((padded - 8 - tokens, width), F32))
    extended = jnp.concatenate(extended, axis=0).astype(BF)
    slot = jnp.concatenate([slot, jnp.full((padded - tokens, lay.experts), -1.0, F32)], axis=0)
    block, place, within, at = lay.split(iota((lay.total, lay.experts), 0))
    of_row = (block * lay.exp_dev + within == iota((lay.total, lay.experts), 1)).astype(F32).astype(BF)
    row_slot = dot_nt(of_row, slot.astype(BF))
    _, place, _, at = lay.split(iota((lay.total, padded), 0))
    wanted = jnp.where(place < lay.slots, at, 1000).astype(F32)
    lane = iota((lay.total, padded), 1)
    off = jnp.where(lane < padded - 8, row_slot - wanted, (place - lay.slots).astype(F32))
    off = jnp.where(lane <= padded - 8, off, 1.0)
    pick = off == 0.0
    out_ref[...] = dot(pick.astype(F32).astype(BF), extended).astype(BF)


def combine_kernel(lay, ids_ref, weights_ref, back_ref, out_ref):
    tokens, top_k = ids_ref.shape
    ids = ids_ref[...]
    mix = weights_ref[...].astype(BF).astype(F32)
    _, slot = positions(ids_ref, lay)
    lanes = iota((tokens, lay.experts), 1)
    weight = jnp.zeros((tokens, lay.experts), F32)
    for s in range(top_k):
        weight = weight + jnp.where(ids[:, s : s + 1] == lanes, mix[:, s : s + 1], 0.0)
    block, place, within, at = lay.split(iota((lay.experts, lay.total), 1))
    of_row = (block * lay.exp_dev + within == iota((lay.experts, lay.total), 0)).astype(F32).astype(BF)
    row_slot = dot(slot.astype(BF), of_row)
    row_weight = dot(weight.astype(BF), of_row)
    _, place, _, at = lay.split(iota((tokens, lay.total), 1))
    wanted = jnp.where(place < lay.slots, at, 1000).astype(F32)
    matrix = jnp.where(row_slot == wanted, row_weight, 0.0).astype(BF)
    out_ref[...] = dot(matrix, back_ref[...]).astype(BF)


def starts_of(counts, lay):
    columns = lay.columns
    before = (iota((columns, columns), 0) < iota((columns, columns), 1)).astype(F32).astype(BF)
    starts, totals, base = [], [], jnp.zeros((8, 1), F32)
    for count in counts:
        starts.append(dot(count.astype(BF), before) + base)
        total = jnp.sum(count, axis=1, keepdims=True)
        totals.append(total)
        base = base + total
    return starts, totals


def spread(values, of_group, product):
    high = jnp.floor(values * (1.0 / 64.0))
    low = values - 64.0 * high
    return product(high.astype(BF), of_group) * 64.0 + product(low.astype(BF), of_group)


def up_kernel(lay, rows, chunk, step_ref, x_ref, gate_ref, upper_ref, meta_ref, loads_ref, *refs):
    exp_dev, width, hidden = gate_ref.shape
    per = rows // PIECE
    out_refs, stage_ref, sems = refs[: 2 * per], refs[2 * per], refs[2 * per + 1]
    me, base = step_ref[0], step_ref[1]
    x = x_ref[...]
    block, place, within, at = lay.split(iota((8, lay.total), 1))
    group_block = lay.split(iota((lay.columns, lay.total), 1))[0]
    of_group = (group_block == iota((lay.columns, lay.total), 0)).astype(F32).astype(BF)
    counts = []
    for w in range(exp_dev):
        lane = (iota((8, width), 1) == me * exp_dev + w).astype(F32).astype(BF)
        seen = jnp.where(place == lay.slots, dot_nt(lane, x), 0.0)
        counts.append(dot_nt(seen.astype(BF), of_group))
    starts, totals = starts_of(counts, lay)
    target = jnp.full((8, lay.total), -1.0, F32)
    for w in range(exp_dev):
        first = spread(starts[w], of_group, dot)
        count = dot(counts[w].astype(BF), of_group)
        here = (within == w) & (place < lay.slots) & (at.astype(F32) < count)
        target = jnp.where(here, first + at.astype(F32), target)
        meta_ref[w * 8 : w * 8 + 8, 0 : lay.columns] = counts[w]
        loads_ref[w] = jnp.sum(totals[w][0:1, 0:1]).astype(jnp.int32)
    every = dot((place == lay.slots).astype(F32).astype(BF), x)
    pair = floor_div(iota((width, 128), 0), exp_dev, width)
    pair = (pair == iota((width, 128), 1)).astype(F32)
    pair = jnp.where(iota((width, 128), 0) < lay.experts, pair, 0.0).astype(BF)
    loads_ref[exp_dev] = jnp.max(spread(every, pair, dot)[0:1, :]).astype(jnp.int32)
    target = target[0:1, :].astype(jnp.int32) - base
    shift = base.astype(F32)
    copies = []
    for first in range(0, rows, chunk):
        size = min(chunk, rows - first)
        pick = (iota((size, lay.total), 0) + first == target).astype(F32).astype(BF)
        picked = dot(pick, x)
        row = (iota((size, width), 0) + first).astype(F32) + shift
        low = jnp.zeros((1, 1), F32)
        parts = []
        for w in range(exp_dev):
            high = low + totals[w][0:1, 0:1]
            parts.append(jnp.where((row >= low) & (row < high), picked, 0.0).astype(BF))
            low = high
        for which, ref in enumerate((gate_ref, upper_ref)):
            total = dot(parts[0], ref[0])
            for w in range(1, exp_dev):
                total = total + dot(parts[w], ref[w])
            stage_ref[which, first : first + size, :] = total.astype(BF)
            for piece in range(first // PIECE, (first + size) // PIECE):
                index = which * per + piece
                copies.append(
                    pltpu.make_async_copy(
                        stage_ref.at[which, pl.ds(piece * PIECE, PIECE)], out_refs[index], sems.at[index]
                    )
                )
                copies[-1].start()
    for copy in copies:
        copy.wait()


def down_kernel(lay, rows, chunk, adds, step_ref, meta_ref, down_ref, *refs):
    exp_dev, hidden, width = down_ref.shape
    per = rows // PIECE
    refs = list(refs)
    before_ref = refs.pop(0) if adds else None
    summed, (out_ref, stage_ref, held_ref, sems) = refs[: 2 * per], refs[2 * per :]
    base = step_ref[1]
    copies = []
    for piece in range(per):
        for which in range(2):
            index = which * per + piece
            copies.append(
                pltpu.make_async_copy(
                    summed[index], stage_ref.at[which, pl.ds(piece * PIECE, PIECE)], sems.at[index]
                )
            )
            copies[-1].start()
    counts = [meta_ref[w * 8 : w * 8 + 8, 0 : lay.columns] for w in range(exp_dev)]
    starts, totals = starts_of(counts, lay)
    shift = base.astype(F32)
    for first in range(0, rows, chunk):
        size = min(chunk, rows - first)
        for copy in copies[2 * (first // PIECE) : 2 * ((first + size) // PIECE)]:
            copy.wait()
        gate = stage_ref[0, first : first + size, :].astype(F32)
        upper = stage_ref[1, first : first + size, :].astype(F32)
        inner = (gate / (1.0 + jnp.exp(-gate)) * upper).astype(BF)
        row = (iota((size, width), 0) + first).astype(F32) + shift
        result = dot(inner, down_ref[0])
        low = totals[0][0:1, 0:1]
        for w in range(1, exp_dev):
            result = jnp.where(row >= low, dot(inner, down_ref[w]), result)
            low = low + totals[w][0:1, 0:1]
        held_ref[first : first + size, :] = result.astype(BF)
    held = held_ref[...]
    step = lay.rows * 4 if lay.columns % 4 == 0 else lay.rows
    for top in range(0, lay.total, step):
        block, place, within, at = lay.split(iota((step, 128), 0) + top)
        group_block = lay.split(iota((step, lay.columns), 0) + top)[0]
        of_group = (group_block == iota((step, lay.columns), 1)).astype(F32).astype(BF)

        def product(values, matrix):
            wide = jnp.broadcast_to(values[0:1, :].astype(F32), (128, lay.columns))
            return dot_nt(matrix, wide.astype(BF))

        target = jnp.full((step, 128), -1.0, F32)
        for w in range(exp_dev):
            start = spread(starts[w], of_group, product)
            count = product(counts[w], of_group)
            here = (within == w) & (place < lay.slots) & (at.astype(F32) < count)
            target = jnp.where(here, start + at.astype(F32), target)
        target = target.astype(jnp.int32) - base
        blocks = []
        for left in range(0, rows, 128):
            wide = min(128, rows - left)
            blocks.append((target[:, :wide] == iota((step, wide), 1) + left).astype(F32).astype(BF))
        pick = jnp.concatenate(blocks, axis=1) if len(blocks) > 1 else blocks[0]
        placed = dot(pick, held)
        if adds:
            placed = placed + before_ref[top : top + step, :].astype(F32)
        out_ref[top : top + step, :] = placed.astype(BF)


def experts(lay, rows, chunk, me, base, before, received, w_gate, w_up, w_down):
    exp_dev, width, hidden = w_gate.shape
    per = rows // PIECE
    vmem = pl.BlockSpec(memory_space=pltpu.VMEM)
    smem = pl.BlockSpec(memory_space=pltpu.SMEM)
    anywhere = pl.BlockSpec(memory_space=pl.ANY)
    step = jnp.stack([me, jnp.asarray(base, jnp.int32)])
    meta, loads, *parts = pl.pallas_call(
        functools.partial(up_kernel, lay, rows, chunk),
        out_shape=[
            jax.ShapeDtypeStruct((8 * exp_dev, 128), F32),
            jax.ShapeDtypeStruct((exp_dev + 1,), jnp.int32),
        ]
        + [jax.ShapeDtypeStruct((PIECE, hidden), BF)] * (2 * per),
        in_specs=[smem, vmem, vmem, vmem],
        out_specs=[vmem, smem] + [anywhere] * (2 * per),
        scratch_shapes=[pltpu.VMEM((2, rows, hidden), BF), pltpu.SemaphoreType.DMA((2 * per,))],
        compiler_params=PARAMS,
        name="up",
    )(step, received, w_gate, w_up)
    summed = lax.psum(parts, "dp")
    adds = before is not None
    out = pl.pallas_call(
        functools.partial(down_kernel, lay, rows, chunk, adds),
        out_shape=jax.ShapeDtypeStruct((lay.total, width), BF),
        in_specs=[smem, vmem, vmem] + [vmem] * adds + [anywhere] * (2 * per),
        out_specs=vmem,
        scratch_shapes=[
            pltpu.VMEM((2, rows, hidden), BF),
            pltpu.VMEM((rows, width), BF),
            pltpu.SemaphoreType.DMA((2 * per,)),
        ],
        compiler_params=PARAMS,
        name="down",
    )(step, meta, w_down, *([before] if adds else []), *summed)
    return out, loads


def body(tokens, route_ids, route_weights, w_gate, w_up, w_down):
    columns = lax.axis_size("expert")
    tok_col, top_k = route_ids.shape
    exp_dev = w_gate.shape[0]
    width = tokens.shape[1]
    capacity = min(tok_col, 3 * tok_col * top_k // (exp_dev * columns))
    lay = Layout(columns, capacity, exp_dev)
    sending = pl.pallas_call(
        functools.partial(dispatch_kernel, lay),
        out_shape=jax.ShapeDtypeStruct((lay.total, width), BF),
        compiler_params=PARAMS,
        name="dispatch",
    )(route_ids, tokens)
    received = lax.all_to_all(
        sending.reshape(columns, lay.rows, width), "expert", split_axis=0, concat_axis=0, tiled=True
    ).reshape(lay.total, width)
    me = lax.axis_index("expert").astype(jnp.int32)
    rows = min(ROWS, columns * lay.slots)
    expert_out, loads = experts(lay, rows, CHUNK, me, 0, None, received, w_gate, w_up, w_down)

    def more(carry):
        return carry[0] < loads[exp_dev]

    def further(carry):
        base, out = carry
        out, _ = experts(lay, rows, CHUNK, me, base, out, received, w_gate, w_up, w_down)
        return base + rows, out

    _, expert_out = lax.while_loop(more, further, (jnp.int32(rows), expert_out))
    returned = lax.all_to_all(
        expert_out.reshape(columns, lay.rows, width), "expert", split_axis=0, concat_axis=0, tiled=True
    ).reshape(lay.total, width)
    combined = pl.pallas_call(
        functools.partial(combine_kernel, lay),
        out_shape=jax.ShapeDtypeStruct((tok_col, width), BF),
        compiler_params=PARAMS,
        name="combine",
    )(route_ids, route_weights, returned)
    return combined, loads[:exp_dev]


def solution(mesh):
    placed = (
        P("expert", "dp"),
        P("expert", None),
        P("expert", None),
        P("expert", "dp", None),
        P("expert", "dp", None),
        P("expert", None, "dp"),
    )
    return jax.shard_map(
        body,
        mesh=mesh,
        in_specs=placed,
        out_specs=(P("expert", "dp"), P("expert")),
        check_vma=False,
    )
```

profile of v0, /device:TPU:1, one launch (start us, length us, event | category | flops | bytes accessed | tf_op | source)
XLA Modules:
  0.0 148.7 jit_solution(3954034647029695383)
XLA Ops:
  0.6 0.0 copy-start.2
  0.6 0.8 copy.9.ids_ref
  1.4 0.0 copy-done.2
  1.4 2.0 %dispatch.1 = bf16[1536,256]{1,0:T(8,128)(2,1)} custom-call(s32[56,8]{1,0:T(8,128)S(1)} %copy.9.ids_ref, bf16[56,256]{1,0:T(8,128)(2,1)S(1)} %copy-done.2), custom_call_target="tpu_custom_call" | custom-call | tf_op jit(solution)/shard_map/dispatch/pallas_call | solution.py:295
  3.5 0.0 copy-done
  3.5 11.2 %all-to-all-start = ((bf16[32,48,256]{2,1,0:T(8,128)(2,1)}), bf16[32,48,256]{2,1,0:T(8,128)(2,1)}, u32[]{:S(2)}, u32[]{:S(2)}) async-start(bf16[32,48,256]{2,1,0:T(8,128)(2,1)} %bitcast.4), calls=%async_computation | async-start | bytes 1572864 | tf_op jit(solution)/shard_map/all_to_all | solution.py:301
  14.7 0.1 pad_add_fusion.1.step_ref
  14.8 14.3 %all-to-all-done = bf16[32,48,256]{2,1,0:T(8,128)(2,1)} async-done(((bf16[32,48,256]{2,1,0:T(8,128)(2,1)}), bf16[32,48,256]{2,1,0:T(8,128)(2,1)}, u32[]{:S(2)}, u32[]{:S(2)}) %all-to-all-start) | async-done | bytes 786464 | tf_op jit(solution)/shard_map/all_to_all | solution.py:301
  29.1 0.0 copy-done.3
  29.1 0.0 copy-done.4
  29.1 10.3 %up.2 = (f32[16,128]{1,0:T(8,128)S(1)}, s32[3]{0:T(128)}, bf16[16,768]{1,0:T(8,128)(2,1)S(1)}, bf16[16,768]{1,0:T(8,128)(2,1)S(1)}, bf16[16,768]{1,0:T(8,128)(2,...) custom-call(s32[2]{0:T(128)S(1)} %pad_add_fusion.1.step_ref, ...), custom_call_target="tpu_custom_call" | custom-call | tf_op jit(solution)/shard_map/up/pallas_call | solution.py:257
  39.4 67.0 %all-reduce.6 = (bf16[16,768]{1,0:T(8,128)(2,1)S(1)}, bf16[16,768]{1,0:T(8,128)(2,1)S(1)}, bf16[16,768]{1,0:T(8,128)(2,1)S(1)}, bf16[16,768]{1,0:T(8,128)(2,1)S(...) all-reduce(bf16[16,768]{1,0:T(8,128)(2,1)S(1)} %get-tuple-element.1, ...), channel_id=1, replica_groups=mesh['dp'=16,'expert'=32] {'dp'}, use_global_device_ids=true, to_apply=%region_0.0 | all-reduce | flops 884736 | bytes 3538944 | tf_op jit(solution)/shard_map/psum | solution.py:270
  106.4 9.4 %down.2 = bf16[1536,256]{1,0:T(8,128)(2,1)} custom-call(s32[2]{0:T(128)S(1)} %pad_add_fusion.1.step_ref, f32[16,128]{1,0:T(8,128)S(1)} %get-tuple-element.192.meta_ref, bf16[2,768,256]{2,1,0:T(8,128)(2,1)} %down_ref.1, bf16[16,768]{1,0:T(8,128)(2,1)S(1)} %get-tuple-element.355.refs_0_, bf16[16,768]{1,0:T(8,128)(2,1)S(1)} %get-tuple-element.356.refs_1_, ...), custom_call_target="tpu_custom_call" | custom-call | tf_op jit(solution)/shard_map/down/pallas_call | solution.py:272
  115.7 1.8 %while.10 = (s32[]{:T(128)}, bf16[1536,256]{1,0:T(8,128)(2,1)}, s32[3]{0:T(128)}, s32[]{:T(128)}, bf16[1536,256]{1,0:T(8,128)(2,1)}, /*index=5*/bf16[2,256,768]{...) while((s32[]{:T(128)}, bf16[1536,256]{1,0:T(8,128)(2,1)}, ...), condition=%wide.region_145.0_spmd, body=%wide.region_72.0_spmd.sunk | while | flops 884740 | bytes 8257757 | solution.py:316
  115.7 0.0 copy-start.7
  115.7 0.6 copy-done.7
  116.4 0.6 slice.7
  117.6 0.0 copy-start.6
  117.6 15.5 %all-to-all-start.1 = ((bf16[32,48,256]{2,1,0:T(8,128)(2,1)}), bf16[32,48,256]{2,1,0:T(8,128)(2,1)S(1)}, u32[]{:S(2)}, u32[]{:S(2)}) async-start(bf16[32,48,256]{2,1,0:T(8,128)(2,1)} %bitcast.15), calls=%async_computation.1 | async-start | bytes 1572864 | tf_op jit(solution)/shard_map/all_to_all | solution.py:317
  133.1 0.0 copy-done.6
  133.1 0.0 copy-start.1
  133.1 0.1 copy.10.weights_ref
  133.2 14.2 %all-to-all-done.1 = bf16[32,48,256]{2,1,0:T(8,128)(2,1)S(1)} async-done(((bf16[32,48,256]{2,1,0:T(8,128)(2,1)}), bf16[32,48,256]{2,1,0:T(8,128)(2,1)S(1)}, u32[]{:S(2)}, u32[]{:S(2)}) %all-to-all-start.1) | async-done | bytes 786464 | tf_op jit(solution)/shard_map/all_to_all | solution.py:317
  147.4 1.3 combine.1
  (4 shorter events, 0.0 us)
Async XLA Ops:
  0.6 0.8 copy-start.2
  1.4 2.1 %copy-start = (s32[56,8]{1,0:T(8,128)}, s32[56,8]{1,0:T(8,128)S(1)}, u32[]{:S(2)}) copy-start(s32[56,8]{1,0:T(8,128)S(1)} %copy.9.ids_ref) | copy-start | bytes 5380
  3.5 25.6 %copy-start.3 = (bf16[2,256,768]{2,1,0:T(8,128)(2,1)S(1)}, bf16[2,256,768]{2,1,0:T(8,128)(2,1)}, u32[]{:S(2)}) copy-start(bf16[2,256,768]{2,1,0:T(8,128)(2,1)} %gate_ref.1) | copy-start | bytes 2359300
  3.5 25.6 %copy-start.4 = (bf16[2,256,768]{2,1,0:T(8,128)(2,1)S(1)}, bf16[2,256,768]{2,1,0:T(8,128)(2,1)}, u32[]{:S(2)}) copy-start(bf16[2,256,768]{2,1,0:T(8,128)(2,1)} %upper_ref.1) | copy-start | bytes 2359300
  3.5 25.6 %all-to-all-start = ((bf16[32,48,256]{2,1,0:T(8,128)(2,1)}), bf16[32,48,256]{2,1,0:T(8,128)(2,1)}, u32[]{:S(2)}, u32[]{:S(2)}) async-start(bf16[32,48,256]{2,1,0:T(8,128)(2,1)} %bitcast.4), calls=%async_computation | async-start | bytes 1572864 | tf_op jit(solution)/shard_map/all_to_all | solution.py:301
  115.7 0.7 copy-start.7
  117.6 15.5 %copy-start.6 = (f32[56,8]{0,1:T(8,128)S(1)}, f32[56,8]{0,1:T(8,128)}, u32[]{:S(2)}) copy-start(f32[56,8]{0,1:T(8,128)} %param.10) | copy-start | bytes 5380
  117.6 29.8 %all-to-all-start.1 = ((bf16[32,48,256]{2,1,0:T(8,128)(2,1)}), bf16[32,48,256]{2,1,0:T(8,128)(2,1)S(1)}, u32[]{:S(2)}, u32[]{:S(2)}) async-start(bf16[32,48,256]{2,1,0:T(8,128)(2,1)} %bitcast.15), calls=%async_computation.1 | async-start | bytes 1572864 | tf_op jit(solution)/shard_map/all_to_all | solution.py:317
  133.1 14.3 %copy-start.1 = (s32[56,8]{1,0:T(8,128)S(1)}, s32[56,8]{1,0:T(8,128)}, u32[]{:S(2)}) copy-start(s32[56,8]{1,0:T(8,128)} %copy-done) | copy-start | bytes 5380
where the time goes:
time: 149 us
  blocking collectives  67 us (45%)
  waiting for transfers between devices  28.5 us (19%)
  starting transfers between devices  26.7 us (18%)
  Pallas kernels  23 us (15%)
  local copies, waits for them, and re-layouts  2.12 us (1%)
    psum x1, blocking collectives, experts(): summed = lax.psum(parts, 'dp')  67 us
    all_to_all x1, starting transfers between devices, body(): lax.all_to_all(expert_out.reshape(columns, lay.rows, width), 'expert', sp...  15.5 us
    all_to_all x1, waiting for transfers between devices, body(): lax.all_to_all(sending.reshape(columns, lay.rows, width), 'expert', split...  14.3 us
    all_to_all x1, waiting for transfers between devices, body(): lax.all_to_all(expert_out.reshape(columns, lay.rows, width), 'expert', sp...  14.2 us
    all_to_all x1, starting transfers between devices, body(): lax.all_to_all(sending.reshape(columns, lay.rows, width), 'expert', split...  11.2 us
    pallas_call x1, Pallas kernels, experts(): pl.pallas_call(functools.partial(up_kernel, lay, rows, chunk), out_shape=...  10.3 us
    pallas_call x1, Pallas kernels, experts(): pl.pallas_call(functools.partial(down_kernel, lay, rows, chunk, adds), ou...  9.37 us
  transfers between devices with their start and end apart: 2, of which 2 were waited for; matrix products, arithmetic and copies ran while one was open for 0% of the time, Pallas kernels for 0%

commit v1 on v0

--- a/solution.py
+++ b/solution.py
@@ -53,14 +53,14 @@
 
 
 def positions(ids_ref, lay):
-    tokens, top_k = ids_ref.shape
+    top_k, tokens = ids_ref.shape
     ids = ids_ref[...]
-    lanes = iota((tokens, lay.experts), 1)
-    chose = jnp.zeros((tokens, lay.experts), F32)
+    of = iota((lay.experts, tokens), 0)
+    chose = jnp.zeros((lay.experts, tokens), F32)
     for s in range(top_k):
-        chose = chose + (ids[:, s : s + 1] == lanes).astype(F32)
-    before = (iota((tokens, tokens), 0) > iota((tokens, tokens), 1)).astype(F32).astype(BF)
-    rank = dot(before, chose.astype(BF))
+        chose = chose + (ids[s : s + 1, :] == of).astype(F32)
+    before = (iota((tokens, tokens), 0) < iota((tokens, tokens), 1)).astype(F32).astype(BF)
+    rank = dot(chose.astype(BF), before)
     return chose, jnp.where(chose > 0, rank, -1.0)
 
 
@@ -69,16 +69,16 @@
     padded = -(-tokens // 8) * 8 + 8
     chose, slot = positions(ids_ref, lay)
     ones = jnp.ones((8, tokens), BF)
-    counts = dot(ones, chose.astype(BF))
+    counts = dot_nt(ones, chose.astype(BF))
     counts = jnp.concatenate([counts, jnp.zeros((8, width - lay.experts), F32)], axis=1)
     extended = [tokens_ref[...].astype(F32), counts]
     if padded - 8 > tokens:
         extended.insert(1, jnp.zeros((padded - 8 - tokens, width), F32))
     extended = jnp.concatenate(extended, axis=0).astype(BF)
-    slot = jnp.concatenate([slot, jnp.full((padded - tokens, lay.experts), -1.0, F32)], axis=0)
+    slot = jnp.concatenate([slot, jnp.full((lay.experts, padded - tokens), -1.0, F32)], axis=1)
     block, place, within, at = lay.split(iota((lay.total, lay.experts), 0))
     of_row = (block * lay.exp_dev + within == iota((lay.total, lay.experts), 1)).astype(F32).astype(BF)
-    row_slot = dot_nt(of_row, slot.astype(BF))
+    row_slot = dot(of_row, slot.astype(BF))
     _, place, _, at = lay.split(iota((lay.total, padded), 0))
     wanted = jnp.where(place < lay.slots, at, 1000).astype(F32)
     lane = iota((lay.total, padded), 1)
@@ -89,18 +89,18 @@
 
 
 def combine_kernel(lay, ids_ref, weights_ref, back_ref, out_ref):
-    tokens, top_k = ids_ref.shape
+    top_k, tokens = ids_ref.shape
     ids = ids_ref[...]
     mix = weights_ref[...].astype(BF).astype(F32)
     _, slot = positions(ids_ref, lay)
-    lanes = iota((tokens, lay.experts), 1)
-    weight = jnp.zeros((tokens, lay.experts), F32)
+    of = iota((lay.experts, tokens), 0)
+    weight = jnp.zeros((lay.experts, tokens), F32)
     for s in range(top_k):
-        weight = weight + jnp.where(ids[:, s : s + 1] == lanes, mix[:, s : s + 1], 0.0)
+        weight = weight + jnp.where(ids[s : s + 1, :] == of, mix[s : s + 1, :], 0.0)
     block, place, within, at = lay.split(iota((lay.experts, lay.total), 1))
     of_row = (block * lay.exp_dev + within == iota((lay.experts, lay.total), 0)).astype(F32).astype(BF)
-    row_slot = dot(slot.astype(BF), of_row)
-    row_weight = dot(weight.astype(BF), of_row)
+    row_slot = dot(slot.T.astype(BF), of_row)
+    row_weight = dot(weight.T.astype(BF), of_row)
     _, place, _, at = lay.split(iota((tokens, lay.total), 1))
     wanted = jnp.where(place < lay.slots, at, 1000).astype(F32)
     matrix = jnp.where(row_slot == wanted, row_weight, 0.0).astype(BF)
@@ -125,10 +125,9 @@
     return product(high.astype(BF), of_group) * 64.0 + product(low.astype(BF), of_group)
 
 
-def up_kernel(lay, rows, chunk, step_ref, x_ref, gate_ref, upper_ref, meta_ref, loads_ref, *refs):
+def up_kernel(lay, rows, chunk, step_ref, x_ref, gate_ref, upper_ref, meta_ref, loads_ref, most_ref, *out_refs):
     exp_dev, width, hidden = gate_ref.shape
     per = rows // PIECE
-    out_refs, stage_ref, sems = refs[: 2 * per], refs[2 * per], refs[2 * per + 1]
     me, base = step_ref[0], step_ref[1]
     x = x_ref[...]
     block, place, within, at = lay.split(iota((8, lay.total), 1))
@@ -152,10 +151,9 @@
     pair = floor_div(iota((width, 128), 0), exp_dev, width)
     pair = (pair == iota((width, 128), 1)).astype(F32)
     pair = jnp.where(iota((width, 128), 0) < lay.experts, pair, 0.0).astype(BF)
-    loads_ref[exp_dev] = jnp.max(spread(every, pair, dot)[0:1, :]).astype(jnp.int32)
+    most_ref[0] = jnp.max(spread(every, pair, dot)[0:1, :]).astype(jnp.int32)
     target = target[0:1, :].astype(jnp.int32) - base
     shift = base.astype(F32)
-    copies = []
     for first in range(0, rows, chunk):
         size = min(chunk, rows - first)
         pick = (iota((size, lay.total), 0) + first == target).astype(F32).astype(BF)
@@ -171,17 +169,11 @@
             total = dot(parts[0], ref[0])
             for w in range(1, exp_dev):
                 total = total + dot(parts[w], ref[w])
-            stage_ref[which, first : first + size, :] = total.astype(BF)
-            for piece in range(first // PIECE, (first + size) // PIECE):
-                index = which * per + piece
-                copies.append(
-                    pltpu.make_async_copy(
-                        stage_ref.at[which, pl.ds(piece * PIECE, PIECE)], out_refs[index], sems.at[index]
-                    )
-                )
-                copies[-1].start()
-    for copy in copies:
-        copy.wait()
+            total = total.astype(BF)
+            for piece in range(size // PIECE):
+                out_refs[which * per + first // PIECE + piece][...] = total[
+                    piece * PIECE : (piece + 1) * PIECE
+                ]
 
 
 def down_kernel(lay, rows, chunk, adds, step_ref, meta_ref, down_ref, *refs):
@@ -189,27 +181,16 @@
     per = rows // PIECE
     refs = list(refs)
     before_ref = refs.pop(0) if adds else None
-    summed, (out_ref, stage_ref, held_ref, sems) = refs[: 2 * per], refs[2 * per :]
+    summed, (out_ref, held_ref) = refs[: 2 * per], refs[2 * per :]
     base = step_ref[1]
-    copies = []
-    for piece in range(per):
-        for which in range(2):
-            index = which * per + piece
-            copies.append(
-                pltpu.make_async_copy(
-                    summed[index], stage_ref.at[which, pl.ds(piece * PIECE, PIECE)], sems.at[index]
-                )
-            )
-            copies[-1].start()
     counts = [meta_ref[w * 8 : w * 8 + 8, 0 : lay.columns] for w in range(exp_dev)]
     starts, totals = starts_of(counts, lay)
     shift = base.astype(F32)
     for first in range(0, rows, chunk):
         size = min(chunk, rows - first)
-        for copy in copies[2 * (first // PIECE) : 2 * ((first + size) // PIECE)]:
-            copy.wait()
-        gate = stage_ref[0, first : first + size, :].astype(F32)
-        upper = stage_ref[1, first : first + size, :].astype(F32)
+        pieces = range(first // PIECE, (first + size) // PIECE)
+        gate = jnp.concatenate([summed[p][...] for p in pieces], axis=0).astype(F32)
+        upper = jnp.concatenate([summed[per + p][...] for p in pieces], axis=0).astype(F32)
         inner = (gate / (1.0 + jnp.exp(-gate)) * upper).astype(BF)
         row = (iota((size, width), 0) + first).astype(F32) + shift
         result = dot(inner, down_ref[0])
@@ -252,18 +233,17 @@
     per = rows // PIECE
     vmem = pl.BlockSpec(memory_space=pltpu.VMEM)
     smem = pl.BlockSpec(memory_space=pltpu.SMEM)
-    anywhere = pl.BlockSpec(memory_space=pl.ANY)
     step = jnp.stack([me, jnp.asarray(base, jnp.int32)])
-    meta, loads, *parts = pl.pallas_call(
+    meta, loads, most, *parts = pl.pallas_call(
         functools.partial(up_kernel, lay, rows, chunk),
         out_shape=[
             jax.ShapeDtypeStruct((8 * exp_dev, 128), F32),
-            jax.ShapeDtypeStruct((exp_dev + 1,), jnp.int32),
+            jax.ShapeDtypeStruct((exp_dev,), jnp.int32),
+            jax.ShapeDtypeStruct((1,), jnp.int32),
         ]
         + [jax.ShapeDtypeStruct((PIECE, hidden), BF)] * (2 * per),
         in_specs=[smem, vmem, vmem, vmem],
-        out_specs=[vmem, smem] + [anywhere] * (2 * per),
-        scratch_shapes=[pltpu.VMEM((2, rows, hidden), BF), pltpu.SemaphoreType.DMA((2 * per,))],
+        out_specs=[vmem, smem, smem] + [vmem] * (2 * per),
         compiler_params=PARAMS,
         name="up",
     )(step, received, w_gate, w_up)
@@ -272,17 +252,13 @@
     out = pl.pallas_call(
         functools.partial(down_kernel, lay, rows, chunk, adds),
         out_shape=jax.ShapeDtypeStruct((lay.total, width), BF),
-        in_specs=[smem, vmem, vmem] + [vmem] * adds + [anywhere] * (2 * per),
+        in_specs=[smem, vmem, vmem] + [vmem] * adds + [vmem] * (2 * per),
         out_specs=vmem,
-        scratch_shapes=[
-            pltpu.VMEM((2, rows, hidden), BF),
-            pltpu.VMEM((rows, width), BF),
-            pltpu.SemaphoreType.DMA((2 * per,)),
-        ],
+        scratch_shapes=[pltpu.VMEM((rows, width), BF)],
         compiler_params=PARAMS,
         name="down",
     )(step, meta, w_down, *([before] if adds else []), *summed)
-    return out, loads
+    return out, loads, most[0]
 
 
 def body(tokens, route_ids, route_weights, w_gate, w_up, w_down):
@@ -297,20 +273,20 @@
         out_shape=jax.ShapeDtypeStruct((lay.total, width), BF),
         compiler_params=PARAMS,
         name="dispatch",
-    )(route_ids, tokens)
+    )(route_ids.T, tokens)
     received = lax.all_to_all(
         sending.reshape(columns, lay.rows, width), "expert", split_axis=0, concat_axis=0, tiled=True
     ).reshape(lay.total, width)
     me = lax.axis_index("expert").astype(jnp.int32)
     rows = min(ROWS, columns * lay.slots)
-    expert_out, loads = experts(lay, rows, CHUNK, me, 0, None, received, w_gate, w_up, w_down)
+    expert_out, loads, most = experts(lay, rows, CHUNK, me, 0, None, received, w_gate, w_up, w_down)
 
     def more(carry):
-        return carry[0] < loads[exp_dev]
+        return carry[0] < most
 
     def further(carry):
         base, out = carry
-        out, _ = experts(lay, rows, CHUNK, me, base, out, received, w_gate, w_up, w_down)
+        out, _, _ = experts(lay, rows, CHUNK, me, base, out, received, w_gate, w_up, w_down)
         return base + rows, out
 
     _, expert_out = lax.while_loop(more, further, (jnp.int32(rows), expert_out))
@@ -322,8 +298,8 @@
         out_shape=jax.ShapeDtypeStruct((tok_col, width), BF),
         compiler_params=PARAMS,
         name="combine",
-    )(route_ids, route_weights, returned)
-    return combined, loads[:exp_dev]
+    )(route_ids.T, route_weights.T, returned)
+    return combined, loads
 
 
 def solution(mesh):

time: 149 us -> 138 us (0.926)
  blocking collectives: 67 us -> 95.9 us
  starting transfers between devices: 26.7 us -> 11.1 us
  waiting for transfers between devices: 28.5 us -> 14.3 us
  Pallas kernels: 23 us -> 12.9 us
    all_to_all x0 -> x1, blocking collectives: none -> 28.9 us  [body(): lax.all_to_all(expert_out.reshape(columns, lay.rows, width), 'expert', sp...]
    all_to_all x1 -> x0, starting transfers between devices: 15.5 us -> none  [body(): lax.all_to_all(expert_out.reshape(columns, lay.rows, width), 'expert', sp...]
    all_to_all x1 -> x0, waiting for transfers between devices: 14.2 us -> none  [body(): lax.all_to_all(expert_out.reshape(columns, lay.rows, width), 'expert', sp...]
    pallas_call x1, Pallas kernels: 10.3 us -> 5.25 us  [experts(): pl.pallas_call(functools.partial(up_kernel, lay, rows, chunk), out_shape=...]
    pallas_call x1, Pallas kernels: 9.37 us -> 4.57 us  [experts(): pl.pallas_call(functools.partial(down_kernel, lay, rows, chunk, adds), ou...]
  transfers between devices with their start and end apart: 2 -> 1, of which waited for: 2 -> 1; matrix products, arithmetic and copies ran while one was open for 0% -> 0% of each run, Pallas kernels for 0% -> 0%
where the time goes in v1:
time: 138 us; the launch traced here: 137 us
  blocking collectives  95.9 us (69%)
  waiting for transfers between devices  14.3 us (10%)
  Pallas kernels  12.9 us (9%)
  starting transfers between devices  11.1 us (8%)
  local copies, waits for them, and re-layouts  1.44 us (1%)
    psum x1, blocking collectives, experts(): summed = lax.psum(parts, 'dp')  67 us
    all_to_all x1, blocking collectives, body(): lax.all_to_all(expert_out.reshape(columns, lay.rows, width), 'expert', sp...  28.9 us
    all_to_all x1, waiting for transfers between devices, body(): lax.all_to_all(sending.reshape(columns, lay.rows, width), 'expert', split...  14.3 us
    all_to_all x1, starting transfers between devices, body(): lax.all_to_all(sending.reshape(columns, lay.rows, width), 'expert', split...  11.1 us
    pallas_call x1, Pallas kernels, experts(): pl.pallas_call(functools.partial(up_kernel, lay, rows, chunk), out_shape=...  5.25 us
    pallas_call x1, Pallas kernels, experts(): pl.pallas_call(functools.partial(down_kernel, lay, rows, chunk, adds), ou...  4.57 us
  transfers between devices with their start and end apart: 1, of which 1 were waited for; matrix products, arithmetic and copies ran while one was open for 0% of the time, Pallas kernels for 0%

profile of v1, /device:TPU:1, one launch (start us, length us, event | category | flops | bytes accessed | tf_op | source)
XLA Modules:
  0.0 137.3 jit_solution(1510752770789293321)
XLA Ops:
  0.6 0.0 copy-start.32
  0.6 0.7 copy-done.32
  1.4 0.0 copy-start.33
  1.4 0.7 copy-done.33
  2.1 1.9 %dispatch.1 = bf16[1536,256]{1,0:T(8,128)(2,1)} custom-call(s32[8,56]{1,0:T(8,128)S(1)} %bitcast.15, bf16[56,256]{1,0:T(8,128)(2,1)S(1)} %copy-done.32), custom_call_target="tpu_custom_call" | custom-call | tf_op jit(solution)/shard_map/dispatch/pallas_call | solution.py:271
  4.0 11.1 %all-to-all-start = ((bf16[32,48,256]{2,1,0:T(8,128)(2,1)}), bf16[32,48,256]{2,1,0:T(8,128)(2,1)}, u32[]{:S(2)}, u32[]{:S(2)}) async-start(bf16[32,48,256]{2,1,0:T(8,128)(2,1)} %bitcast.5), calls=%async_computation | async-start | bytes 1572864 | tf_op jit(solution)/shard_map/all_to_all | solution.py:277
  15.1 0.1 pad_add_fusion.1.step_ref
  15.1 14.3 %all-to-all-done = bf16[32,48,256]{2,1,0:T(8,128)(2,1)} async-done(((bf16[32,48,256]{2,1,0:T(8,128)(2,1)}), bf16[32,48,256]{2,1,0:T(8,128)(2,1)}, u32[]{:S(2)}, u32[]{:S(2)}) %all-to-all-start) | async-done | bytes 786464 | tf_op jit(solution)/shard_map/all_to_all | solution.py:277
  29.5 5.2 %up.2 = (f32[16,128]{1,0:T(8,128)S(1)}, s32[2]{0:T(128)}, s32[1]{0:T(128)}, bf16[16,768]{1,0:T(8,128)(2,1)S(1)}, bf16[16,768]{1,0:T(8,128)(2,1)S(1)}, /*index=5*...) custom-call(s32[2]{0:T(128)S(1)} %pad_add_fusion.1.step_ref, ...), custom_call_target="tpu_custom_call" | custom-call | tf_op jit(solution)/shard_map/up/pallas_call | solution.py:237
  34.7 67.0 %all-reduce.6 = (bf16[16,768]{1,0:T(8,128)(2,1)S(1)}, bf16[16,768]{1,0:T(8,128)(2,1)S(1)}, bf16[16,768]{1,0:T(8,128)(2,1)S(1)}, bf16[16,768]{1,0:T(8,128)(2,1)S(...) all-reduce(bf16[16,768]{1,0:T(8,128)(2,1)S(1)} %get-tuple-element.1, ...), channel_id=1, replica_groups=mesh['dp'=16,'expert'=32] {'dp'}, use_global_device_ids=true, to_apply=%region_0.0 | all-reduce | flops 884736 | bytes 3538944 | tf_op jit(solution)/shard_map/psum | solution.py:250
  101.7 4.6 %down.2 = bf16[1536,256]{1,0:T(8,128)(2,1)S(1)} custom-call(s32[2]{0:T(128)S(1)} %pad_add_fusion.1.step_ref, f32[16,128]{1,0:T(8,128)S(1)} %get-tuple-element.193.meta_ref, bf16[2,768,256]{2,1,0:T(8,128)(2,1)} %down_ref.1, bf16[16,768]{1,0:T(8,128)(2,1)S(1)} %get-tuple-element.357.refs_0_, bf16[16,768]{1,0:T(8,128)(2,1)S(1)} %get-tuple-element.358.refs_1_, ...), custom_call_target="tpu_custom_call" | custom-call | tf_op jit(solution)/shard_map/down/pallas_call | solution.py:252
  106.3 0.8 while.10
  107.1 0.0 copy-start.34
  107.1 0.0 copy-start.35
  107.1 28.9 %all_to_all.10 = bf16[32,48,256]{2,1,0:T(8,128)(2,1)S(1)} all-to-all(bf16[32,48,256]{2,1,0:T(8,128)(2,1)S(1)} %bitcast.18), channel_id=1, replica_groups=mesh['dp'=16,'expert'=32] {'expert'}, dimensions={0} | all-to-all | bytes 1572864 | tf_op jit(solution)/shard_map/all_to_all | solution.py:293
  136.0 0.0 copy-done.34
  136.0 0.0 copy-done.35
  136.0 1.2 combine.1
Async XLA Ops:
  0.6 0.7 copy-start.32
  1.4 0.7 copy-start.33
  4.0 25.5 %all-to-all-start = ((bf16[32,48,256]{2,1,0:T(8,128)(2,1)}), bf16[32,48,256]{2,1,0:T(8,128)(2,1)}, u32[]{:S(2)}, u32[]{:S(2)}) async-start(bf16[32,48,256]{2,1,0:T(8,128)(2,1)} %bitcast.5), calls=%async_computation | async-start | bytes 1572864 | tf_op jit(solution)/shard_map/all_to_all | solution.py:277
  107.1 28.9 %copy-start.34 = (s32[56,8]{0,1:T(8,128)S(1)}, s32[56,8]{0,1:T(8,128)}, u32[]{:S(2)}) copy-start(s32[56,8]{0,1:T(8,128)} %param.9) | copy-start | bytes 5380
  107.1 28.9 %copy-start.35 = (f32[56,8]{0,1:T(8,128)S(1)}, f32[56,8]{0,1:T(8,128)}, u32[]{:S(2)}) copy-start(f32[56,8]{0,1:T(8,128)} %param.10) | copy-start | bytes 5380

commit v2 on v1

v2 whole, which is shorter than its diff:
```python
import functools

import jax
import jax.numpy as jnp
import numpy as np
from jax import lax
from jax.experimental import pallas as pl
from jax.experimental.pallas import tpu as pltpu
from jax.sharding import PartitionSpec as P

BF = jnp.bfloat16
F32 = jnp.float32
PIECE = 16
ROWS = 576
CHUNK = 192
NT = (((1,), (1,)), ((), ()))
PARAMS = pltpu.CompilerParams(vmem_limit_bytes=24 * 1024 * 1024)


def dot(a, b):
    return jnp.dot(a, b, preferred_element_type=F32)


def dot_nt(a, b):
    return lax.dot_general(a, b, NT, preferred_element_type=F32)


def iota(shape, dim):
    return lax.broadcasted_iota(jnp.int32, shape, dim)


FREE, COUNTS = 90, 100


class Layout:
    def __init__(self, columns, capacity, exp_dev):
        self.columns, self.capacity, self.exp_dev = columns, capacity, exp_dev
        self.sub = -(-(capacity + 1) // 8) * 8
        self.rows = -(-(self.sub * exp_dev) // 16) * 16
        self.total = columns * self.rows
        self.experts = columns * exp_dev
        self.wide = -(-(self.experts + 1) // 128) * 128
        row = np.arange(self.total)
        group, place = row // self.rows, row % self.rows
        within = np.minimum(place // self.sub, exp_dev - 1)
        at = place - within * self.sub
        at = np.where(at < capacity, at, np.where((at == capacity) & (within == 0), COUNTS, FREE))
        table = np.zeros((self.total, self.wide), np.float32)
        table[row, within * columns + group] = 1.0
        table[:, self.experts] = -at
        self.table = table

    def expert_ids(self, shape, dim):
        at = iota(shape, dim)
        ids = at * self.exp_dev
        for w in range(1, self.exp_dev):
            ids = ids - jnp.where(at >= w * self.columns, self.experts - 1, 0)
        return ids


def chosen(ids_ref, lay):
    top_k, tokens = ids_ref.shape
    ids = ids_ref[...]
    of = lay.expert_ids((lay.experts, tokens), 0)
    chose = jnp.zeros((lay.experts, tokens), F32)
    for s in range(top_k):
        chose = chose + (ids[s : s + 1, :] == of).astype(F32)
    before = (iota((tokens, tokens), 0) < iota((tokens, tokens), 1)).astype(F32).astype(BF)
    rank = dot(chose.astype(BF), before)
    return chose, jnp.where(chose > 0, rank, -1.0)


def dispatch_kernel(lay, ids_ref, tokens_ref, table_ref, out_ref):
    tokens, width = tokens_ref.shape
    real = -(-tokens // 8) * 8
    chose, slot = chosen(ids_ref, lay)
    counts = dot_nt(jnp.ones((8, tokens), BF), chose.astype(BF))
    counts = jnp.concatenate([counts, jnp.zeros((8, width - lay.experts), F32)], axis=1)
    extended = [tokens_ref[...].astype(F32), counts]
    if real > tokens:
        extended.insert(1, jnp.zeros((real - tokens, width), F32))
    extended = jnp.concatenate(extended, axis=0).astype(BF)
    extra = jnp.where(iota((lay.experts, real + 8 - tokens), 1) == real - tokens, float(COUNTS), -1.0)
    slot = jnp.concatenate([slot, extra], axis=1)
    ones = (iota((lay.wide - lay.experts, real + 8), 0) == 0).astype(F32)
    slot = jnp.concatenate([slot, ones], axis=0).astype(BF)
    pick = (dot(table_ref[...], slot) == 0.0).astype(F32).astype(BF)
    out_ref[...] = dot(pick, extended).astype(BF)


def mix_kernel(lay, ids_ref, weights_ref, across_ref, *refs):
    n = (len(refs) - 2) // 2
    sources, out_ref, held, sems = refs[:n], refs[n], refs[n + 1 : 2 * n + 1], refs[2 * n + 1]
    copies = [pltpu.make_async_copy(a, b, sems.at[i]) for i, (a, b) in enumerate(zip(sources, held))]
    for copy in copies:
        copy.start()
    top_k, tokens = ids_ref.shape
    ids = ids_ref[...]
    mix = weights_ref[...].astype(BF).astype(F32)
    _, slot = chosen(ids_ref, lay)
    of = lay.expert_ids((lay.experts, tokens), 0)
    weight = jnp.zeros((lay.experts, tokens), F32)
    for s in range(top_k):
        weight = weight + jnp.where(ids[s : s + 1, :] == of, mix[s : s + 1, :], 0.0)
    rest = (tokens, lay.wide - lay.experts)
    slot = jnp.concatenate([slot.T, (iota(rest, 1) == 0).astype(F32)], axis=1).astype(BF)
    weight = jnp.concatenate([weight.T, jnp.zeros(rest, F32)], axis=1).astype(BF)
    across = across_ref[...]
    out_ref[...] = jnp.where(dot(slot, across) == 0.0, dot(weight, across), 0.0).astype(BF)
    for copy in copies:
        copy.wait()


def combine_kernel(matrix_ref, back_ref, out_ref):
    out_ref[...] = dot(matrix_ref[...], back_ref[...]).astype(BF)


def starts_of(counts, lay):
    i, k = iota((lay.wide, lay.wide), 0), iota((lay.wide, lay.wide), 1)
    start = dot(counts.astype(BF), (i < k).astype(F32).astype(BF))
    start = jnp.where(iota(start.shape, 1) < lay.experts, start, 0.0)
    high = jnp.floor(start * (1.0 / 64.0))
    return high, start - 64.0 * high


def ends_of(counts, lay):
    lane = iota((1, lay.wide), 1)
    return [
        jnp.sum(jnp.where(lane < (w + 1) * lay.columns, counts[0:1], 0.0), axis=1, keepdims=True)
        for w in range(lay.exp_dev)
    ]


def up_kernel(lay, rows, chunk, step_ref, x_ref, gate_ref, upper_ref, across_ref, meta_ref, loads_ref, most_ref, *out_refs):
    exp_dev, width, hidden = gate_ref.shape
    per = rows // PIECE
    me, base = step_ref[0], step_ref[1]
    x = x_ref[...]
    across = across_ref[...]
    of_group = jnp.where(
        across_ref[lay.experts : lay.experts + 16, :].astype(F32)[0:1, :] == float(-COUNTS),
        across_ref[0 : lay.columns, :].astype(F32),
        0.0,
    ).astype(BF)
    every = dot(of_group, x).astype(BF)
    own = []
    for w in range(exp_dev):
        lane = (iota((8, width), 1) == w * lay.columns + me).astype(F32).astype(BF)
        own.append(dot_nt(lane, every))
    own.append(jnp.zeros((8, lay.wide - lay.experts), F32))
    counts = jnp.concatenate(own, axis=1)
    meta_ref[...] = counts
    high, low = starts_of(counts, lay)
    ends = ends_of(counts, lay)
    lane, row = iota((8, lay.wide), 1), iota((8, lay.wide), 0)
    low = jnp.where(lane == lay.experts, -1.0, low)
    room = jnp.where(lane == lay.experts, 1.0, counts)
    terms = jnp.where(row == 0, high, jnp.where(row == 1, low, room)).astype(BF)
    spread = dot(terms, across)
    target = jnp.where(spread[2:3] > 0.0, 64.0 * spread[0:1] + spread[1:2], -1.0)
    target = target.astype(jnp.int32) - base
    shift = base.astype(F32)
    for first in range(0, rows, chunk):
        size = min(chunk, rows - first)
        pick = (iota((size, lay.total), 0) + first == target).astype(F32).astype(BF)
        picked = dot(pick, x)
        row = (iota((size, width), 0) + first).astype(F32) + shift
        begin = jnp.zeros((1, 1), F32)
        parts = []
        for w in range(exp_dev):
            parts.append(jnp.where((row >= begin) & (row < ends[w]), picked, 0.0).astype(BF))
            begin = ends[w]
        for which, ref in enumerate((gate_ref, upper_ref)):
            total = dot(parts[0], ref[0])
            for w in range(1, exp_dev):
                total = total + dot(parts[w], ref[w])
            total = total.astype(BF)
            for piece in range(size // PIECE):
                out_refs[which * per + first // PIECE + piece][...] = total[
                    piece * PIECE : (piece + 1) * PIECE
                ]
    loads = dot(jnp.ones((8, lay.columns), BF), every)[0:1]
    begin = 0.0
    for w in range(exp_dev):
        loads_ref[w] = (jnp.sum(ends[w]) - begin).astype(jnp.int32)
        begin = jnp.sum(ends[w])
    lane = iota((1, width), 1)
    full = loads
    for w in range(1, exp_dev):
        full = full + pltpu.roll(loads, width - w * lay.columns, axis=1)
    most_ref[0] = jnp.max(jnp.where(lane < lay.columns, full, 0.0)).astype(jnp.int32)


def down_kernel(lay, rows, chunk, adds, step_ref, meta_ref, down_ref, table_ref, *refs):
    exp_dev, hidden, width = down_ref.shape
    per = rows // PIECE
    refs = list(refs)
    before_ref = refs.pop(0) if adds else None
    summed, (out_ref, held_ref) = refs[: 2 * per], refs[2 * per :]
    base = step_ref[1]
    counts = meta_ref[...]
    high, low = starts_of(counts, lay)
    ends = ends_of(counts, lay)
    lane = iota((8, lay.wide), 1)
    low = jnp.where(lane == lay.experts, -1.0, low)
    room = jnp.where(lane == lay.experts, 1.0, counts)
    high, low, room = (jnp.broadcast_to(v[0:1], (128, lay.wide)).astype(BF) for v in (high, low, room))
    shift = base.astype(F32)
    for first in range(0, rows, chunk):
        size = min(chunk, rows - first)
        pieces = range(first // PIECE, (first + size) // PIECE)
        gate = jnp.concatenate([summed[p][...] for p in pieces], axis=0).astype(F32)
        upper = jnp.concatenate([summed[per + p][...] for p in pieces], axis=0).astype(F32)
        inner = (gate / (1.0 + jnp.exp(-gate)) * upper).astype(BF)
        row = (iota((size, width), 0) + first).astype(F32) + shift
        result = dot(inner, down_ref[0])
        for w in range(1, exp_dev):
            result = jnp.where(row >= ends[w - 1], dot(inner, down_ref[w]), result)
        held_ref[first : first + size, :] = result.astype(BF)
    held = held_ref[...]
    step = lay.rows * 4 if lay.columns % 4 == 0 else lay.rows
    for top in range(0, lay.total, step):
        table = table_ref[top : top + step, :]
        target = 64.0 * dot_nt(table, high) + dot_nt(table, low)
        target = jnp.where(dot_nt(table, room) > 0.0, target, -1.0).astype(jnp.int32) - base
        blocks = []
        for left in range(0, rows, 128):
            wide = min(128, rows - left)
            blocks.append((target[:, :wide] == iota((step, wide), 1) + left).astype(F32).astype(BF))
        pick = jnp.concatenate(blocks, axis=1) if len(blocks) > 1 else blocks[0]
        placed = dot(pick, held)
        if adds:
            placed = placed + before_ref[top : top + step, :].astype(F32)
        out_ref[top : top + step, :] = placed.astype(BF)


def experts(lay, rows, chunk, me, base, before, received, w_gate, w_up, w_down):
    exp_dev, width, hidden = w_gate.shape
    per = rows // PIECE
    vmem = pl.BlockSpec(memory_space=pltpu.VMEM)
    smem = pl.BlockSpec(memory_space=pltpu.SMEM)
    step = jnp.stack([me, jnp.asarray(base, jnp.int32)])
    meta, loads, most, *parts = pl.pallas_call(
        functools.partial(up_kernel, lay, rows, chunk),
        out_shape=[
            jax.ShapeDtypeStruct((8, lay.wide), F32),
            jax.ShapeDtypeStruct((exp_dev,), jnp.int32),
            jax.ShapeDtypeStruct((1,), jnp.int32),
        ]
        + [jax.ShapeDtypeStruct((PIECE, hidden), BF)] * (2 * per),
        in_specs=[smem] + [vmem] * 4,
        out_specs=[vmem, smem, smem] + [vmem] * (2 * per),
        compiler_params=PARAMS,
        name="up",
    )(step, received, w_gate, w_up, jnp.asarray(lay.table.T, BF))
    summed = lax.psum(parts, "dp")
    adds = before is not None
    out = pl.pallas_call(
        functools.partial(down_kernel, lay, rows, chunk, adds),
        out_shape=jax.ShapeDtypeStruct((lay.total, width), BF),
        in_specs=[smem] + [vmem] * (3 + adds + 2 * per),
        out_specs=vmem,
        scratch_shapes=[pltpu.VMEM((rows, width), BF)],
        compiler_params=PARAMS,
        name="down",
    )(step, meta, w_down, jnp.asarray(lay.table, BF), *([before] if adds else []), *summed)
    return out, loads, most[0]


def body(tokens, route_ids, route_weights, w_gate, w_up, w_down):
    columns = lax.axis_size("expert")
    tok_col, top_k = route_ids.shape
    exp_dev = w_gate.shape[0]
    width = tokens.shape[1]
    capacity = min(tok_col, 3 * tok_col * top_k // (exp_dev * columns))
    lay = Layout(columns, capacity, exp_dev)
    sending = pl.pallas_call(
        functools.partial(dispatch_kernel, lay),
        out_shape=jax.ShapeDtypeStruct((lay.total, width), BF),
        compiler_params=PARAMS,
        name="dispatch",
    )(route_ids.T, tokens, jnp.asarray(lay.table, BF))
    received = lax.all_to_all(
        sending.reshape(columns, lay.rows, width), "expert", split_axis=0, concat_axis=0, tiled=True
    ).reshape(lay.total, width)
    vmem = pl.BlockSpec(memory_space=pltpu.VMEM)
    weights = (w_gate, w_up)
    matrix, *near = pl.pallas_call(
        functools.partial(mix_kernel, lay),
        out_shape=[jax.ShapeDtypeStruct((tok_col, lay.total), BF)]
        + [jax.ShapeDtypeStruct(w.shape, w.dtype) for w in weights],
        in_specs=[vmem] * 3 + [pl.BlockSpec(memory_space=pl.ANY)] * 2,
        out_specs=[vmem] * 3,
        scratch_shapes=[pltpu.SemaphoreType.DMA((2,))],
        compiler_params=PARAMS,
        name="mix",
    )(route_ids.T, route_weights.T, jnp.asarray(lay.table.T, BF), *weights)
    me = lax.axis_index("expert").astype(jnp.int32)
    rows = min(ROWS, columns * exp_dev * capacity)
    expert_out, loads, most = experts(lay, rows, CHUNK, me, 0, None, received, *near, w_down)

    def more(carry):
        return carry[0] < most

    def further(carry):
        base, out = carry
        out, _, _ = experts(lay, rows, CHUNK, me, base, out, received, w_gate, w_up, w_down)
        return base + rows, out

    _, expert_out = lax.while_loop(more, further, (jnp.int32(rows), expert_out))
    returned = lax.all_to_all(
        expert_out.reshape(columns, lay.rows, width), "expert", split_axis=0, concat_axis=0, tiled=True
    ).reshape(lay.total, width)
    combined = pl.pallas_call(
        combine_kernel,
        out_shape=jax.ShapeDtypeStruct((tok_col, width), BF),
        compiler_params=PARAMS,
        name="combine",
    )(matrix, returned)
    return combined, loads


def solution(mesh):
    placed = (
        P("expert", "dp"),
        P("expert", None),
        P("expert", None),
        P("expert", "dp", None),
        P("expert", "dp", None),
        P("expert", None, "dp"),
    )
    return jax.shard_map(
        body,
        mesh=mesh,
        in_specs=placed,
        out_specs=(P("expert", "dp"), P("expert")),
        check_vma=False,
    )
```

time: 138 us -> 138 us (level)
  waiting for transfers between devices: 14.3 us -> 10.6 us
  Pallas kernels: 12.9 us -> 14.8 us
    all_to_all x1, waiting for transfers between devices: 14.3 us -> 10.6 us  [body(): lax.all_to_all(sending.reshape(columns, lay.rows, width), 'expert', split...]
    pallas_call x1 -> x2, Pallas kernels: 1.24 us -> 3.25 us  [the longest x1 2.38 us: body(): pl.pallas_call(functools.partial(mix_kernel, lay), out_shape=[jax.ShapeDt...]
    unnamed x8 -> x12, local copies, waits for them, and re-layouts: 1.44 us -> 2.77 us
  transfers between devices with their start and end apart: 1 -> 1, of which waited for: 1 -> 1; matrix products, arithmetic and copies ran while one was open for 0% -> 0% of each run, Pallas kernels for 0% -> 2%
where the time goes in v2:
time: 138 us; the launch traced here: 137 us
  blocking collectives  96.3 us (70%)
  Pallas kernels  14.8 us (11%)
  starting transfers between devices  11.1 us (8%)
  waiting for transfers between devices  10.6 us (8%)
  local copies, waits for them, and re-layouts  2.77 us (2%)
    psum x1, blocking collectives, experts(): summed = lax.psum(parts, 'dp')  67.1 us
    all_to_all x1, blocking collectives, body(): lax.all_to_all(expert_out.reshape(columns, lay.rows, width), 'expert', sp...  29.2 us
    all_to_all x1, starting transfers between devices, body(): lax.all_to_all(sending.reshape(columns, lay.rows, width), 'expert', split...  11.1 us
    all_to_all x1, waiting for transfers between devices, body(): lax.all_to_all(sending.reshape(columns, lay.rows, width), 'expert', split...  10.6 us
    pallas_call x1, Pallas kernels, experts(): pl.pallas_call(functools.partial(up_kernel, lay, rows, chunk), out_shape=...  5.26 us
    pallas_call x1, Pallas kernels, experts(): pl.pallas_call(functools.partial(down_kernel, lay, rows, chunk, adds), ou...  3.68 us
    unnamed x12, local copies, waits for them, and re-layouts  2.77 us
  transfers between devices with their start and end apart: 1, of which 1 were waited for; matrix products, arithmetic and copies ran while one was open for 0% of the time, Pallas kernels for 2%

profile of v2, /device:TPU:1, one launch (start us, length us, event | category | flops | bytes accessed | tf_op | source)
XLA Modules:
  0.0 137.2 jit_solution(8694889164602663162)
XLA Ops:
  0.6 0.0 copy-start.34
  0.6 0.7 copy-done.34
  1.4 0.0 copy-start.35
  1.4 0.7 copy-done.35
  2.1 2.6 %dispatch.1 = bf16[1536,256]{1,0:T(8,128)(2,1)} custom-call(s32[8,56]{1,0:T(8,128)S(1)} %bitcast.15, bf16[56,256]{1,0:T(8,128)(2,1)S(1)} %copy-done.34, bf16[1536,128]{1,0:T(8,128)(2,1)} %constant.14.clone.table_ref), custom_call_target="tpu_custom_call" | custom-call | tf_op jit(solution)/shard_map/dispatch/pallas_call | solution.py:277
  4.7 11.1 %all-to-all-start = ((bf16[32,48,256]{2,1,0:T(8,128)(2,1)}), bf16[32,48,256]{2,1,0:T(8,128)(2,1)}, u32[]{:S(2)}, u32[]{:S(2)}) async-start(bf16[32,48,256]{2,1,0:T(8,128)(2,1)} %bitcast.3), calls=%async_computation | async-start | bytes 1572864 | tf_op jit(solution)/shard_map/all_to_all | solution.py:283
  15.8 0.0 copy-start.37
  15.8 0.0 copy-start.36
  15.8 0.7 copy-done.37
  16.5 0.0 copy-done.36
  16.5 2.4 %mix.1 = (bf16[56,1536]{1,0:T(8,128)(2,1)S(1)}, bf16[2,256,768]{2,1,0:T(8,128)(2,1)S(1)}, bf16[2,256,768]{2,1,0:T(8,128)(2,1)S(1)}) custom-call(s32[8,56]{1,0:T(8,128)S(1)} %bitcast.16, f32[8,56]{1,0:T(8,128)S(1)} %bitcast.17, bf16[128,1536]{1,0:T(8,128)(2,1)} %constant.15.clone.across_ref, bf16[2,256,768]{2,1,0:T(8,128)(2,1)} %refs_0_.1, ...), custom_call_target="tpu_custom_call" | custom-call | tf_op jit(solution)/shard_map/mix/pallas_call | solution.py:288
  18.9 0.0 copy-start.32
  18.9 0.7 copy-done.32
  19.6 0.1 pad_add_fusion.1.step_ref
  19.6 10.6 %all-to-all-done = bf16[32,48,256]{2,1,0:T(8,128)(2,1)} async-done(((bf16[32,48,256]{2,1,0:T(8,128)(2,1)}), bf16[32,48,256]{2,1,0:T(8,128)(2,1)}, u32[]{:S(2)}, u32[]{:S(2)}) %all-to-all-start) | async-done | bytes 786464 | tf_op jit(solution)/shard_map/all_to_all | solution.py:283
  30.2 5.3 %up.2 = (f32[8,128]{1,0:T(8,128)S(1)}, s32[2]{0:T(128)}, s32[1]{0:T(128)}, bf16[16,768]{1,0:T(8,128)(2,1)S(1)}, bf16[16,768]{1,0:T(8,128)(2,1)S(1)}, /*index=5*/...) custom-call(s32[2]{0:T(128)S(1)} %pad_add_fusion.1.step_ref, ...), custom_call_target="tpu_custom_call" | custom-call | tf_op jit(solution)/shard_map/up/pallas_call | solution.py:243
  35.5 67.1 %all-reduce.6 = (bf16[16,768]{1,0:T(8,128)(2,1)S(1)}, bf16[16,768]{1,0:T(8,128)(2,1)S(1)}, bf16[16,768]{1,0:T(8,128)(2,1)S(1)}, bf16[16,768]{1,0:T(8,128)(2,1)S(...) all-reduce(bf16[16,768]{1,0:T(8,128)(2,1)S(1)} %get-tuple-element.2, ...), channel_id=1, replica_groups=mesh['dp'=16,'expert'=32] {'dp'}, use_global_device_ids=true, to_apply=%region_0.0 | all-reduce | flops 884736 | bytes 3538944 | tf_op jit(solution)/shard_map/psum | solution.py:256
  102.6 3.7 %down.2 = bf16[1536,256]{1,0:T(8,128)(2,1)S(1)} custom-call(s32[2]{0:T(128)S(1)} %pad_add_fusion.1.step_ref, f32[8,128]{1,0:T(8,128)S(1)} %get-tuple-element.209.meta_ref, bf16[2,768,256]{2,1,0:T(8,128)(2,1)} %down_ref.1, bf16[1536,128]{1,0:T(8,128)(2,1)} %constant.14.clone.table_ref, bf16[16,768]{1,0:T(8,128)(2,1)S(1)} %get-tuple-element.549.refs_0_, ...), custom_call_target="tpu_custom_call" | custom-call | tf_op jit(solution)/shard_map/down/pallas_call | solution.py:258
  106.3 0.9 while.11
  107.1 0.0 copy-start.33
  107.1 29.2 %all_to_all.10 = bf16[32,48,256]{2,1,0:T(8,128)(2,1)S(1)} all-to-all(bf16[32,48,256]{2,1,0:T(8,128)(2,1)S(1)} %bitcast.18), channel_id=1, replica_groups=mesh['dp'=16,'expert'=32] {'expert'}, dimensions={0} | all-to-all | bytes 1572864 | tf_op jit(solution)/shard_map/all_to_all | solution.py:311
  136.3 0.0 copy-done.33
  136.3 0.9 combine.1
Async XLA Ops:
  0.6 0.7 copy-start.34
  1.4 0.7 copy-start.35
  4.7 25.5 %all-to-all-start = ((bf16[32,48,256]{2,1,0:T(8,128)(2,1)}), bf16[32,48,256]{2,1,0:T(8,128)(2,1)}, u32[]{:S(2)}, u32[]{:S(2)}) async-start(bf16[32,48,256]{2,1,0:T(8,128)(2,1)} %bitcast.3), calls=%async_computation | async-start | bytes 1572864 | tf_op jit(solution)/shard_map/all_to_all | solution.py:283
  15.8 0.7 copy-start.37
  15.8 0.7 copy-start.36
  18.9 0.7 copy-start.32
  107.1 29.2 %copy-start.33 = (bf16[56,1536]{1,0:T(8,128)(2,1)S(1)}, bf16[56,1536]{1,0:T(8,128)(2,1)}, u32[]{:S(2)}) copy-start(bf16[56,1536]{1,0:T(8,128)(2,1)} %copy-done.32) | copy-start | bytes 516100

commit v3 on v2

--- a/solution.py
+++ b/solution.py
@@ -12,7 +12,7 @@
 F32 = jnp.float32
 PIECE = 16
 ROWS = 576
-CHUNK = 192
+CHUNK = 576
 NT = (((1,), (1,)), ((), ()))
 PARAMS = pltpu.CompilerParams(vmem_limit_bytes=24 * 1024 * 1024)
 
@@ -70,12 +70,21 @@
     return chose, jnp.where(chose > 0, rank, -1.0)
 
 
-def dispatch_kernel(lay, ids_ref, tokens_ref, table_ref, out_ref):
+def dispatch_kernel(lay, ids_from, tokens_from, table_from, out_ref, ids_ref, tokens_ref, table_ref, sems):
+    copies = [
+        pltpu.make_async_copy(ids_from, ids_ref, sems.at[0]),
+        pltpu.make_async_copy(tokens_from, tokens_ref, sems.at[1]),
+        pltpu.make_async_copy(table_from, table_ref, sems.at[2]),
+    ]
+    for copy in copies:
+        copy.start()
+    copies[0].wait()
     tokens, width = tokens_ref.shape
     real = -(-tokens // 8) * 8
     chose, slot = chosen(ids_ref, lay)
     counts = dot_nt(jnp.ones((8, tokens), BF), chose.astype(BF))
     counts = jnp.concatenate([counts, jnp.zeros((8, width - lay.experts), F32)], axis=1)
+    copies[1].wait()
     extended = [tokens_ref[...].astype(F32), counts]
     if real > tokens:
         extended.insert(1, jnp.zeros((real - tokens, width), F32))
@@ -84,16 +93,12 @@
     slot = jnp.concatenate([slot, extra], axis=1)
     ones = (iota((lay.wide - lay.experts, real + 8), 0) == 0).astype(F32)
     slot = jnp.concatenate([slot, ones], axis=0).astype(BF)
+    copies[2].wait()
     pick = (dot(table_ref[...], slot) == 0.0).astype(F32).astype(BF)
     out_ref[...] = dot(pick, extended).astype(BF)
 
 
-def mix_kernel(lay, ids_ref, weights_ref, across_ref, *refs):
-    n = (len(refs) - 2) // 2
-    sources, out_ref, held, sems = refs[:n], refs[n], refs[n + 1 : 2 * n + 1], refs[2 * n + 1]
-    copies = [pltpu.make_async_copy(a, b, sems.at[i]) for i, (a, b) in enumerate(zip(sources, held))]
-    for copy in copies:
-        copy.start()
+def mix_kernel(lay, ids_ref, weights_ref, across_ref, out_ref):
     top_k, tokens = ids_ref.shape
     ids = ids_ref[...]
     mix = weights_ref[...].astype(BF).astype(F32)
@@ -107,8 +112,6 @@
     weight = jnp.concatenate([weight.T, jnp.zeros(rest, F32)], axis=1).astype(BF)
     across = across_ref[...]
     out_ref[...] = jnp.where(dot(slot, across) == 0.0, dot(weight, across), 0.0).astype(BF)
-    for copy in copies:
-        copy.wait()
 
 
 def combine_kernel(matrix_ref, back_ref, out_ref):
@@ -159,6 +162,16 @@
     spread = dot(terms, across)
     target = jnp.where(spread[2:3] > 0.0, 64.0 * spread[0:1] + spread[1:2], -1.0)
     target = target.astype(jnp.int32) - base
+    loads = dot(jnp.ones((8, lay.columns), BF), every)[0:1]
+    begin = 0.0
+    for w in range(exp_dev):
+        loads_ref[w] = (jnp.sum(ends[w]) - begin).astype(jnp.int32)
+        begin = jnp.sum(ends[w])
+    lanes = iota((1, width), 1)
+    full = loads
+    for w in range(1, exp_dev):
+        full = full + pltpu.roll(loads, width - w * lay.columns, axis=1)
+    most_ref[0] = jnp.max(jnp.where(lanes < lay.columns, full, 0.0)).astype(jnp.int32)
     shift = base.astype(F32)
     for first in range(0, rows, chunk):
         size = min(chunk, rows - first)
@@ -170,25 +183,13 @@
         for w in range(exp_dev):
             parts.append(jnp.where((row >= begin) & (row < ends[w]), picked, 0.0).astype(BF))
             begin = ends[w]
+        parts = jnp.concatenate(parts, axis=1)
         for which, ref in enumerate((gate_ref, upper_ref)):
-            total = dot(parts[0], ref[0])
-            for w in range(1, exp_dev):
-                total = total + dot(parts[w], ref[w])
-            total = total.astype(BF)
+            total = dot(parts, ref[...].reshape(exp_dev * width, hidden)).astype(BF)
             for piece in range(size // PIECE):
                 out_refs[which * per + first // PIECE + piece][...] = total[
                     piece * PIECE : (piece + 1) * PIECE
                 ]
-    loads = dot(jnp.ones((8, lay.columns), BF), every)[0:1]
-    begin = 0.0
-    for w in range(exp_dev):
-        loads_ref[w] = (jnp.sum(ends[w]) - begin).astype(jnp.int32)
-        begin = jnp.sum(ends[w])
-    lane = iota((1, width), 1)
-    full = loads
-    for w in range(1, exp_dev):
-        full = full + pltpu.roll(loads, width - w * lay.columns, axis=1)
-    most_ref[0] = jnp.max(jnp.where(lane < lay.columns, full, 0.0)).astype(jnp.int32)
 
 
 def down_kernel(lay, rows, chunk, adds, step_ref, meta_ref, down_ref, table_ref, *refs):
@@ -256,7 +257,7 @@
     summed = lax.psum(parts, "dp")
     adds = before is not None
     out = pl.pallas_call(
-        functools.partial(down_kernel, lay, rows, chunk, adds),
+        functools.partial(down_kernel, lay, rows, min(chunk, 192), adds),
         out_shape=jax.ShapeDtypeStruct((lay.total, width), BF),
         in_specs=[smem] + [vmem] * (3 + adds + 2 * per),
         out_specs=vmem,
@@ -265,6 +266,29 @@
         name="down",
     )(step, meta, w_down, jnp.asarray(lay.table, BF), *([before] if adds else []), *summed)
     return out, loads, most[0]
+
+
+def dispatch(lay, route_ids, tokens):
+    tok_col, width = tokens.shape
+    top_k = route_ids.shape[1]
+    table = jnp.asarray(lay.table, BF)
+    sending = pl.pallas_call(
+        functools.partial(dispatch_kernel, lay),
+        out_shape=jax.ShapeDtypeStruct((lay.total, width), BF),
+        in_specs=[pl.BlockSpec(memory_space=pl.ANY)] * 3,
+        out_specs=pl.BlockSpec(memory_space=pltpu.VMEM),
+        scratch_shapes=[
+            pltpu.VMEM((top_k, tok_col), jnp.int32),
+            pltpu.VMEM((tok_col, width), BF),
+            pltpu.VMEM(table.shape, BF),
+            pltpu.SemaphoreType.DMA((3,)),
+        ],
+        compiler_params=PARAMS,
+        name="dispatch",
+    )(route_ids.T, tokens, table)
+    return lax.all_to_all(
+        sending.reshape(lay.columns, lay.rows, width), "expert", split_axis=0, concat_axis=0, tiled=True
+    ).reshape(lay.total, width)
 
 
 def body(tokens, route_ids, route_weights, w_gate, w_up, w_down):
@@ -274,37 +298,24 @@
     width = tokens.shape[1]
     capacity = min(tok_col, 3 * tok_col * top_k // (exp_dev * columns))
     lay = Layout(columns, capacity, exp_dev)
-    sending = pl.pallas_call(
-        functools.partial(dispatch_kernel, lay),
-        out_shape=jax.ShapeDtypeStruct((lay.total, width), BF),
-        compiler_params=PARAMS,
-        name="dispatch",
-    )(route_ids.T, tokens, jnp.asarray(lay.table, BF))
-    received = lax.all_to_all(
-        sending.reshape(columns, lay.rows, width), "expert", split_axis=0, concat_axis=0, tiled=True
-    ).reshape(lay.total, width)
-    vmem = pl.BlockSpec(memory_space=pltpu.VMEM)
-    weights = (w_gate, w_up)
-    matrix, *near = pl.pallas_call(
+    received = dispatch(lay, route_ids, tokens)
+    matrix = pl.pallas_call(
         functools.partial(mix_kernel, lay),
-        out_shape=[jax.ShapeDtypeStruct((tok_col, lay.total), BF)]
-        + [jax.ShapeDtypeStruct(w.shape, w.dtype) for w in weights],
-        in_specs=[vmem] * 3 + [pl.BlockSpec(memory_space=pl.ANY)] * 2,
-        out_specs=[vmem] * 3,
-        scratch_shapes=[pltpu.SemaphoreType.DMA((2,))],
+        out_shape=jax.ShapeDtypeStruct((tok_col, lay.total), BF),
         compiler_params=PARAMS,
         name="mix",
-    )(route_ids.T, route_weights.T, jnp.asarray(lay.table.T, BF), *weights)
+    )(route_ids.T, route_weights.T, jnp.asarray(lay.table.T, BF))
     me = lax.axis_index("expert").astype(jnp.int32)
     rows = min(ROWS, columns * exp_dev * capacity)
-    expert_out, loads, most = experts(lay, rows, CHUNK, me, 0, None, received, *near, w_down)
+    expert_out, loads, most = experts(lay, rows, CHUNK, me, 0, None, received, w_gate, w_up, w_down)
 
     def more(carry):
         return carry[0] < most
 
     def further(carry):
         base, out = carry
-        out, _, _ = experts(lay, rows, CHUNK, me, base, out, received, w_gate, w_up, w_down)
+        again = dispatch(lay, *lax.optimization_barrier((route_ids, tokens, base))[:2])
+        out, _, _ = experts(lay, rows, CHUNK, me, base, out, again, w_gate, w_up, w_down)
         return base + rows, out
 
     _, expert_out = lax.while_loop(more, further, (jnp.int32(rows), expert_out))

time: 138 us -> 136 us (0.986)
  blocking collectives: 96.3 us -> 67.7 us
  waiting for transfers between devices: 10.6 us -> 28.1 us
  starting transfers between devices: 11.1 us -> 25.5 us
  local copies, waits for them, and re-layouts: 2.77 us -> 0.03 us
  Pallas kernels: 14.8 us -> 13 us
    all_to_all x1 -> x0, blocking collectives: 29.2 us -> none  [body(): lax.all_to_all(expert_out.reshape(columns, lay.rows, width), 'expert', sp...]
    all_to_all x1 -> x2, waiting for transfers between devices: 10.6 us -> 28.1 us  [the longest x1 14.3 us: dispatch(): lax.all_to_all(sending.reshape(lay.columns, lay.rows, width), 'expert', s...]
    all_to_all x1 -> x2, starting transfers between devices: 11.1 us -> 25.5 us  [the longest x1 14.9 us: body(): lax.all_to_all(expert_out.reshape(columns, lay.rows, width), 'expert', sp...]
    unnamed x12 -> x10, local copies, waits for them, and re-layouts: 2.77 us -> 0.03 us
  transfers between devices with their start and end apart: 1 -> 2, of which waited for: 1 -> 2; matrix products, arithmetic and copies ran while one was open for 0% -> 0% of each run, Pallas kernels for 2% -> 0%
where the time goes in v3:
time: 136 us
  blocking collectives  67.7 us (50%)
  waiting for transfers between devices  28.1 us (21%)
  starting transfers between devices  25.5 us (19%)
  Pallas kernels  13 us (10%)
    psum x1, blocking collectives, experts(): summed = lax.psum(parts, 'dp')  67.7 us
    all_to_all x1, starting transfers between devices, body(): lax.all_to_all(expert_out.reshape(columns, lay.rows, width), 'expert', sp...  14.9 us
    all_to_all x1, waiting for transfers between devices, dispatch(): lax.all_to_all(sending.reshape(lay.columns, lay.rows, width), 'expert', s...  14.3 us
    all_to_all x1, waiting for transfers between devices, body(): lax.all_to_all(expert_out.reshape(columns, lay.rows, width), 'expert', sp...  13.8 us
    all_to_all x1, starting transfers between devices, dispatch(): lax.all_to_all(sending.reshape(lay.columns, lay.rows, width), 'expert', s...  10.6 us
    pallas_call x1, Pallas kernels, experts(): pl.pallas_call(functools.partial(down_kernel, lay, rows, min(chunk, 192),...  4.59 us
    pallas_call x1, Pallas kernels, experts(): pl.pallas_call(functools.partial(up_kernel, lay, rows, chunk), out_shape=...  4.53 us
  transfers between devices with their start and end apart: 2, of which 2 were waited for; matrix products, arithmetic and copies ran while one was open for 0% of the time, Pallas kernels for 0%

profile of v3, /device:TPU:1, one launch (start us, length us, event | category | flops | bytes accessed | tf_op | source)
XLA Modules:
  0.0 135.9 jit_solution(11758730388060443669)
XLA Ops:
  0.6 2.6 %dispatch.2 = bf16[1536,256]{1,0:T(8,128)(2,1)} custom-call(s32[8,56]{1,0:T(8,128)} %bitcast.27, bf16[56,256]{1,0:T(8,128)(2,1)} %tokens_from.1, bf16[1536,128]{1,0:T(8,128)(2,1)} %constant.14.clone.table_from.table_ref), custom_call_target="tpu_custom_call" | custom-call | tf_op jit(solution)/shard_map/dispatch/pallas_call | solution.py:275
  3.2 0.0 copy-start.33
  3.2 10.6 %all-to-all-start.1 = ((bf16[32,48,256]{2,1,0:T(8,128)(2,1)}), bf16[32,48,256]{2,1,0:T(8,128)(2,1)S(1)}, u32[]{:S(2)}, u32[]{:S(2)}) async-start(bf16[32,48,256]{2,1,0:T(8,128)(2,1)} %bitcast.3), calls=%async_computation.1 | async-start | bytes 1572864 | tf_op jit(solution)/shard_map/all_to_all | solution.py:289
  13.8 0.1 pad_add_fusion.1.step_ref
  13.9 14.3 %all-to-all-done.1 = bf16[32,48,256]{2,1,0:T(8,128)(2,1)S(1)} async-done(((bf16[32,48,256]{2,1,0:T(8,128)(2,1)}), bf16[32,48,256]{2,1,0:T(8,128)(2,1)S(1)}, u32[]{:S(2)}, u32[]{:S(2)}) %all-to-all-start.1) | async-done | bytes 786464 | tf_op jit(solution)/shard_map/all_to_all | solution.py:289
  28.1 0.0 copy-done.33
  28.1 4.5 %up.2 = (f32[8,128]{1,0:T(8,128)S(1)}, s32[2]{0:T(128)}, s32[1]{0:T(128)}, bf16[16,768]{1,0:T(8,128)(2,1)S(1)}, bf16[16,768]{1,0:T(8,128)(2,1)S(1)}, /*index=5*/...) custom-call(s32[2]{0:T(128)S(1)} %pad_add_fusion.1.step_ref, ...), custom_call_target="tpu_custom_call" | custom-call | tf_op jit(solution)/shard_map/up/pallas_call | solution.py:244
  32.7 67.7 %all-reduce.6 = (bf16[16,768]{1,0:T(8,128)(2,1)S(1)}, bf16[16,768]{1,0:T(8,128)(2,1)S(1)}, bf16[16,768]{1,0:T(8,128)(2,1)S(1)}, bf16[16,768]{1,0:T(8,128)(2,1)S(...) all-reduce(bf16[16,768]{1,0:T(8,128)(2,1)S(1)} %get-tuple-element.2, ...), channel_id=1, replica_groups=mesh['dp'=16,'expert'=32] {'dp'}, use_global_device_ids=true, to_apply=%region_0.0 | all-reduce | flops 884736 | bytes 3538944 | tf_op jit(solution)/shard_map/psum | solution.py:257
  100.4 0.0 copy-start.35
  100.4 0.0 copy-start.37
  100.4 4.6 %down.2 = bf16[1536,256]{1,0:T(8,128)(2,1)} custom-call(s32[2]{0:T(128)S(1)} %pad_add_fusion.1.step_ref, f32[8,128]{1,0:T(8,128)S(1)} %get-tuple-element.215.meta_ref, bf16[2,768,256]{2,1,0:T(8,128)(2,1)} %down_ref.1, bf16[1536,128]{1,0:T(8,128)(2,1)} %constant.14.clone.table_from.table_ref, bf16[16,768]{1,0:T(8,128)(2,1)S(1)} %get-tuple-element.667.refs_0_, ...), custom_call_target="tpu_custom_call" | custom-call | tf_op jit(solution)/shard_map/down/pallas_call | solution.py:259
  105.0 0.0 copy-done.35
  105.0 0.0 copy-done.37
  105.0 0.7 while.12
  105.8 0.0 copy-start.32
  105.8 0.0 copy-start.34
  105.8 14.9 %all-to-all-start.2 = ((bf16[32,48,256]{2,1,0:T(8,128)(2,1)}), bf16[32,48,256]{2,1,0:T(8,128)(2,1)S(1)}, u32[]{:S(2)}, u32[]{:S(2)}) async-start(bf16[32,48,256]{2,1,0:T(8,128)(2,1)} %bitcast.6), calls=%async_computation.2 | async-start | bytes 1572864 | tf_op jit(solution)/shard_map/all_to_all | solution.py:322
  120.7 0.0 copy-done.32
  120.7 0.0 copy-done.34
  120.7 0.5 mix.1.matrix_ref
  121.2 13.8 %all-to-all-done.2 = bf16[32,48,256]{2,1,0:T(8,128)(2,1)S(1)} async-done(((bf16[32,48,256]{2,1,0:T(8,128)(2,1)}), bf16[32,48,256]{2,1,0:T(8,128)(2,1)S(1)}, u32[]{:S(2)}, u32[]{:S(2)}) %all-to-all-start.2) | async-done | bytes 786464 | tf_op jit(solution)/shard_map/all_to_all | solution.py:322
  135.0 0.9 combine.1
Async XLA Ops:
  3.2 24.9 %copy-start.33 = (bf16[2,256,768]{2,1,0:T(8,128)(2,1)S(1)}, bf16[2,256,768]{2,1,0:T(8,128)(2,1)}, u32[]{:S(2)}) copy-start(bf16[2,256,768]{2,1,0:T(8,128)(2,1)} %gate_ref.1) | copy-start | bytes 2359300
  3.2 24.9 %all-to-all-start.1 = ((bf16[32,48,256]{2,1,0:T(8,128)(2,1)}), bf16[32,48,256]{2,1,0:T(8,128)(2,1)S(1)}, u32[]{:S(2)}, u32[]{:S(2)}) async-start(bf16[32,48,256]{2,1,0:T(8,128)(2,1)} %bitcast.3), calls=%async_computation.1 | async-start | bytes 1572864 | tf_op jit(solution)/shard_map/all_to_all | solution.py:289
  100.4 4.6 %copy-start.35 = (bf16[56,256]{1,0:T(8,128)(2,1)S(1)}, bf16[56,256]{1,0:T(8,128)(2,1)}, u32[]{:S(2)}) copy-start(bf16[56,256]{1,0:T(8,128)(2,1)} %tokens_from.1) | copy-start | bytes 86020
  100.4 4.6 %copy-start.37 = (s32[56,8]{0,1:T(8,128)S(1)}, s32[56,8]{0,1:T(8,128)}, u32[]{:S(2)}) copy-start(s32[56,8]{0,1:T(8,128)} %param.16) | copy-start | bytes 5380
  105.8 15.0 %copy-start.32 = (f32[56,8]{0,1:T(8,128)S(1)}, f32[56,8]{0,1:T(8,128)}, u32[]{:S(2)}) copy-start(f32[56,8]{0,1:T(8,128)} %param.17) | copy-start | bytes 5380
  105.8 15.0 %copy-start.34 = (bf16[128,1536]{1,0:T(8,128)(2,1)S(1)}, bf16[128,1536]{1,0:T(8,128)(2,1)}, u32[]{:S(2)}) copy-start(bf16[128,1536]{1,0:T(8,128)(2,1)} %get-tuple-element.1140) | copy-start | bytes 1179652
  105.8 29.2 %all-to-all-start.2 = ((bf16[32,48,256]{2,1,0:T(8,128)(2,1)}), bf16[32,48,256]{2,1,0:T(8,128)(2,1)S(1)}, u32[]{:S(2)}, u32[]{:S(2)}) async-start(bf16[32,48,256]{2,1,0:T(8,128)(2,1)} %bitcast.6), calls=%async_computation.2 | async-start | bytes 1572864 | tf_op jit(solution)/shard_map/all_to_all | solution.py:322

commit v4 on v3

--- a/solution.py
+++ b/solution.py
@@ -50,6 +50,11 @@
         table[:, self.experts] = -at
         self.table = table
 
+    def parts(self):
+        groups = next(n for n in (8, 4, 2, 1) if self.columns % n == 0)
+        size = self.rows * groups
+        return [pl.ds(top, size) for top in range(0, self.total, size)]
+
     def expert_ids(self, shape, dim):
         at = iota(shape, dim)
         ids = at * self.exp_dev
@@ -70,7 +75,7 @@
     return chose, jnp.where(chose > 0, rank, -1.0)
 
 
-def dispatch_kernel(lay, ids_from, tokens_from, table_from, out_ref, ids_ref, tokens_ref, table_ref, sems):
+def dispatch_kernel(lay, ids_from, tokens_from, table_from, out_to, ids_ref, tokens_ref, table_ref, out_ref, sems):
     copies = [
         pltpu.make_async_copy(ids_from, ids_ref, sems.at[0]),
         pltpu.make_async_copy(tokens_from, tokens_ref, sems.at[1]),
@@ -94,8 +99,14 @@
     ones = (iota((lay.wide - lay.experts, real + 8), 0) == 0).astype(F32)
     slot = jnp.concatenate([slot, ones], axis=0).astype(BF)
     copies[2].wait()
-    pick = (dot(table_ref[...], slot) == 0.0).astype(F32).astype(BF)
-    out_ref[...] = dot(pick, extended).astype(BF)
+    copies = []
+    for part in lay.parts():
+        pick = (dot(table_ref[part, :], slot) == 0.0).astype(F32).astype(BF)
+        out_ref[part, :] = dot(pick, extended).astype(BF)
+        copies.append(pltpu.make_async_copy(out_ref.at[part], out_to.at[part], sems.at[3 + len(copies)]))
+        copies[-1].start()
+    for copy in copies:
+        copy.wait()
 
 
 def mix_kernel(lay, ids_ref, weights_ref, across_ref, out_ref):
@@ -192,12 +203,18 @@
                 ]
 
 
-def down_kernel(lay, rows, chunk, adds, step_ref, meta_ref, down_ref, table_ref, *refs):
-    exp_dev, hidden, width = down_ref.shape
+def down_kernel(lay, rows, chunk, adds, step_ref, meta_ref, down_from, table_from, *refs):
+    exp_dev, hidden, width = down_from.shape
     per = rows // PIECE
     refs = list(refs)
     before_ref = refs.pop(0) if adds else None
-    summed, (out_ref, held_ref) = refs[: 2 * per], refs[2 * per :]
+    summed, (out_to, held_ref, down_ref, table_ref, out_ref, sems) = refs[: 2 * per], refs[2 * per :]
+    arriving = [
+        pltpu.make_async_copy(down_from, down_ref, sems.at[0]),
+        pltpu.make_async_copy(table_from, table_ref, sems.at[1]),
+    ]
+    for copy in arriving:
+        copy.start()
     base = step_ref[1]
     counts = meta_ref[...]
     high, low = starts_of(counts, lay)
@@ -214,14 +231,18 @@
         upper = jnp.concatenate([summed[per + p][...] for p in pieces], axis=0).astype(F32)
         inner = (gate / (1.0 + jnp.exp(-gate)) * upper).astype(BF)
         row = (iota((size, width), 0) + first).astype(F32) + shift
+        if first == 0:
+            arriving[0].wait()
         result = dot(inner, down_ref[0])
         for w in range(1, exp_dev):
             result = jnp.where(row >= ends[w - 1], dot(inner, down_ref[w]), result)
         held_ref[first : first + size, :] = result.astype(BF)
     held = held_ref[...]
-    step = lay.rows * 4 if lay.columns % 4 == 0 else lay.rows
-    for top in range(0, lay.total, step):
-        table = table_ref[top : top + step, :]
+    arriving[1].wait()
+    leaving = []
+    for part in lay.parts():
+        step = part.size
+        table = table_ref[part, :]
         target = 64.0 * dot_nt(table, high) + dot_nt(table, low)
         target = jnp.where(dot_nt(table, room) > 0.0, target, -1.0).astype(jnp.int32) - base
         blocks = []
@@ -231,8 +252,12 @@
         pick = jnp.concatenate(blocks, axis=1) if len(blocks) > 1 else blocks[0]
         placed = dot(pick, held)
         if adds:
-            placed = placed + before_ref[top : top + step, :].astype(F32)
-        out_ref[top : top + step, :] = placed.astype(BF)
+            placed = placed + before_ref[part, :].astype(F32)
+        out_ref[part, :] = placed.astype(BF)
+        leaving.append(pltpu.make_async_copy(out_ref.at[part], out_to.at[part], sems.at[2 + len(leaving)]))
+        leaving[-1].start()
+    for copy in leaving:
+        copy.wait()
 
 
 def experts(lay, rows, chunk, me, base, before, received, w_gate, w_up, w_down):
@@ -240,6 +265,7 @@
     per = rows // PIECE
     vmem = pl.BlockSpec(memory_space=pltpu.VMEM)
     smem = pl.BlockSpec(memory_space=pltpu.SMEM)
+    anywhere = pl.BlockSpec(memory_space=pl.ANY)
     step = jnp.stack([me, jnp.asarray(base, jnp.int32)])
     meta, loads, most, *parts = pl.pallas_call(
         functools.partial(up_kernel, lay, rows, chunk),
@@ -259,9 +285,15 @@
     out = pl.pallas_call(
         functools.partial(down_kernel, lay, rows, min(chunk, 192), adds),
         out_shape=jax.ShapeDtypeStruct((lay.total, width), BF),
-        in_specs=[smem] + [vmem] * (3 + adds + 2 * per),
-        out_specs=vmem,
-        scratch_shapes=[pltpu.VMEM((rows, width), BF)],
+        in_specs=[smem, vmem, anywhere, anywhere] + [vmem] * (adds + 2 * per),
+        out_specs=anywhere,
+        scratch_shapes=[
+            pltpu.VMEM((rows, width), BF),
+            pltpu.VMEM(w_down.shape, BF),
+            pltpu.VMEM(lay.table.shape, BF),
+            pltpu.VMEM((lay.total, width), BF),
+            pltpu.SemaphoreType.DMA((2 + len(lay.parts()),)),
+        ],
         compiler_params=PARAMS,
         name="down",
     )(step, meta, w_down, jnp.asarray(lay.table, BF), *([before] if adds else []), *summed)
@@ -276,12 +308,13 @@
         functools.partial(dispatch_kernel, lay),
         out_shape=jax.ShapeDtypeStruct((lay.total, width), BF),
         in_specs=[pl.BlockSpec(memory_space=pl.ANY)] * 3,
-        out_specs=pl.BlockSpec(memory_space=pltpu.VMEM),
+        out_specs=pl.BlockSpec(memory_space=pl.ANY),
         scratch_shapes=[
             pltpu.VMEM((top_k, tok_col), jnp.int32),
             pltpu.VMEM((tok_col, width), BF),
             pltpu.VMEM(table.shape, BF),
-            pltpu.SemaphoreType.DMA((3,)),
+            pltpu.VMEM((lay.total, width), BF),
+            pltpu.SemaphoreType.DMA((3 + len(lay.parts()),)),
         ],
         compiler_params=PARAMS,
         name="dispatch",

time: 136 us -> 136 us (level)
  no operation moved by 1% of the time
where the time goes in v4:
time: 136 us
  blocking collectives  67.7 us (50%)
  waiting for transfers between devices  28.1 us (21%)
  starting transfers between devices  25.6 us (19%)
  Pallas kernels  13 us (10%)
    psum x1, blocking collectives, experts(): summed = lax.psum(parts, 'dp')  67.7 us
    all_to_all x1, starting transfers between devices, body(): lax.all_to_all(expert_out.reshape(columns, lay.rows, width), 'expert', sp...  15 us
    all_to_all x1, waiting for transfers between devices, dispatch(): lax.all_to_all(sending.reshape(lay.columns, lay.rows, width), 'expert', s...  14.3 us
    all_to_all x1, waiting for transfers between devices, body(): lax.all_to_all(expert_out.reshape(columns, lay.rows, width), 'expert', sp...  13.8 us
    all_to_all x1, starting transfers between devices, dispatch(): lax.all_to_all(sending.reshape(lay.columns, lay.rows, width), 'expert', s...  10.6 us
    pallas_call x1, Pallas kernels, experts(): pl.pallas_call(functools.partial(down_kernel, lay, rows, min(chunk, 192),...  4.63 us
    pallas_call x1, Pallas kernels, experts(): pl.pallas_call(functools.partial(up_kernel, lay, rows, chunk), out_shape=...  4.53 us
  transfers between devices with their start and end apart: 2, of which 2 were waited for; matrix products, arithmetic and copies ran while one was open for 0% of the time, Pallas kernels for 0%

profile of v4, /device:TPU:1, one launch (start us, length us, event | category | flops | bytes accessed | tf_op | source)
XLA Modules:
  0.0 135.9 jit_solution(7878077399977876867)
XLA Ops:
  0.6 2.5 %dispatch.2 = bf16[1536,256]{1,0:T(8,128)(2,1)} custom-call(s32[8,56]{1,0:T(8,128)} %bitcast.27, bf16[56,256]{1,0:T(8,128)(2,1)} %tokens_from.1, bf16[1536,128]{1,0:T(8,128)(2,1)} %constant.14.clone.table_from), custom_call_target="tpu_custom_call" | custom-call | tf_op jit(solution)/shard_map/dispatch/pallas_call | solution.py:307
  3.1 0.0 copy-start.33
  3.1 10.6 %all-to-all-start.1 = ((bf16[32,48,256]{2,1,0:T(8,128)(2,1)}), bf16[32,48,256]{2,1,0:T(8,128)(2,1)S(1)}, u32[]{:S(2)}, u32[]{:S(2)}) async-start(bf16[32,48,256]{2,1,0:T(8,128)(2,1)} %bitcast.3), calls=%async_computation.1 | async-start | bytes 1572864 | tf_op jit(solution)/shard_map/all_to_all | solution.py:322
  13.7 0.1 pad_add_fusion.1.step_ref
  13.8 14.3 %all-to-all-done.1 = bf16[32,48,256]{2,1,0:T(8,128)(2,1)S(1)} async-done(((bf16[32,48,256]{2,1,0:T(8,128)(2,1)}), bf16[32,48,256]{2,1,0:T(8,128)(2,1)S(1)}, u32[]{:S(2)}, u32[]{:S(2)}) %all-to-all-start.1) | async-done | bytes 786464 | tf_op jit(solution)/shard_map/all_to_all | solution.py:322
  28.0 0.0 copy-done.33
  28.0 4.5 %up.2 = (f32[8,128]{1,0:T(8,128)S(1)}, s32[2]{0:T(128)}, s32[1]{0:T(128)}, bf16[16,768]{1,0:T(8,128)(2,1)S(1)}, bf16[16,768]{1,0:T(8,128)(2,1)S(1)}, /*index=5*/...) custom-call(s32[2]{0:T(128)S(1)} %pad_add_fusion.1.step_ref, ...), custom_call_target="tpu_custom_call" | custom-call | tf_op jit(solution)/shard_map/up/pallas_call | solution.py:270
  32.6 67.7 %all-reduce.6 = (bf16[16,768]{1,0:T(8,128)(2,1)S(1)}, bf16[16,768]{1,0:T(8,128)(2,1)S(1)}, bf16[16,768]{1,0:T(8,128)(2,1)S(1)}, bf16[16,768]{1,0:T(8,128)(2,1)S(...) all-reduce(bf16[16,768]{1,0:T(8,128)(2,1)S(1)} %get-tuple-element.2, ...), channel_id=1, replica_groups=mesh['dp'=16,'expert'=32] {'dp'}, use_global_device_ids=true, to_apply=%region_0.0 | all-reduce | flops 884736 | bytes 3538944 | tf_op jit(solution)/shard_map/psum | solution.py:283
  100.3 0.0 copy-start.35
  100.3 0.0 copy-start.37
  100.3 4.6 %down.2 = bf16[1536,256]{1,0:T(8,128)(2,1)} custom-call(s32[2]{0:T(128)S(1)} %pad_add_fusion.1.step_ref, f32[8,128]{1,0:T(8,128)S(1)} %get-tuple-element.215.meta_ref, bf16[2,768,256]{2,1,0:T(8,128)(2,1)} %down_from.1, bf16[1536,128]{1,0:T(8,128)(2,1)} %constant.14.clone.table_from, bf16[16,768]{1,0:T(8,128)(2,1)S(1)} %get-tuple-element.667.refs_0_, ...), custom_call_target="tpu_custom_call" | custom-call | tf_op jit(solution)/shard_map/down/pallas_call | solution.py:285
  104.9 0.0 copy-done.35
  105.0 0.0 copy-done.37
  105.0 0.7 while.12
  105.7 0.0 copy-start.32
  105.7 0.0 copy-start.34
  105.7 15.0 %all-to-all-start.2 = ((bf16[32,48,256]{2,1,0:T(8,128)(2,1)}), bf16[32,48,256]{2,1,0:T(8,128)(2,1)S(1)}, u32[]{:S(2)}, u32[]{:S(2)}) async-start(bf16[32,48,256]{2,1,0:T(8,128)(2,1)} %bitcast.6), calls=%async_computation.2 | async-start | bytes 1572864 | tf_op jit(solution)/shard_map/all_to_all | solution.py:355
  120.7 0.0 copy-done.32
  120.7 0.0 copy-done.34
  120.7 0.5 mix.1.matrix_ref
  121.2 13.8 %all-to-all-done.2 = bf16[32,48,256]{2,1,0:T(8,128)(2,1)S(1)} async-done(((bf16[32,48,256]{2,1,0:T(8,128)(2,1)}), bf16[32,48,256]{2,1,0:T(8,128)(2,1)S(1)}, u32[]{:S(2)}, u32[]{:S(2)}) %all-to-all-start.2) | async-done | bytes 786464 | tf_op jit(solution)/shard_map/all_to_all | solution.py:355
  135.1 0.9 combine.1
Async XLA Ops:
  3.1 24.9 %copy-start.33 = (bf16[2,256,768]{2,1,0:T(8,128)(2,1)S(1)}, bf16[2,256,768]{2,1,0:T(8,128)(2,1)}, u32[]{:S(2)}) copy-start(bf16[2,256,768]{2,1,0:T(8,128)(2,1)} %gate_ref.1) | copy-start | bytes 2359300
  3.1 24.9 %all-to-all-start.1 = ((bf16[32,48,256]{2,1,0:T(8,128)(2,1)}), bf16[32,48,256]{2,1,0:T(8,128)(2,1)S(1)}, u32[]{:S(2)}, u32[]{:S(2)}) async-start(bf16[32,48,256]{2,1,0:T(8,128)(2,1)} %bitcast.3), calls=%async_computation.1 | async-start | bytes 1572864 | tf_op jit(solution)/shard_map/all_to_all | solution.py:322
  100.3 4.7 %copy-start.35 = (bf16[56,256]{1,0:T(8,128)(2,1)S(1)}, bf16[56,256]{1,0:T(8,128)(2,1)}, u32[]{:S(2)}) copy-start(bf16[56,256]{1,0:T(8,128)(2,1)} %tokens_from.1) | copy-start | bytes 86020
  100.3 4.7 %copy-start.37 = (s32[56,8]{0,1:T(8,128)S(1)}, s32[56,8]{0,1:T(8,128)}, u32[]{:S(2)}) copy-start(s32[56,8]{0,1:T(8,128)} %param.16) | copy-start | bytes 5380
  105.7 15.0 %copy-start.32 = (f32[56,8]{0,1:T(8,128)S(1)}, f32[56,8]{0,1:T(8,128)}, u32[]{:S(2)}) copy-start(f32[56,8]{0,1:T(8,128)} %param.17) | copy-start | bytes 5380
  105.7 15.0 %copy-start.34 = (bf16[128,1536]{1,0:T(8,128)(2,1)S(1)}, bf16[128,1536]{1,0:T(8,128)(2,1)}, u32[]{:S(2)}) copy-start(bf16[128,1536]{1,0:T(8,128)(2,1)} %get-tuple-element.1140) | copy-start | bytes 1179652
  105.7 29.3 %all-to-all-start.2 = ((bf16[32,48,256]{2,1,0:T(8,128)(2,1)}), bf16[32,48,256]{2,1,0:T(8,128)(2,1)S(1)}, u32[]{:S(2)}, u32[]{:S(2)}) async-start(bf16[32,48,256]{2,1,0:T(8,128)(2,1)} %bitcast.6), calls=%async_computation.2 | async-start | bytes 1572864 | tf_op jit(solution)/shard_map/all_to_all | solution.py:355

commit v5 on v4

--- a/solution.py
+++ b/solution.py
@@ -11,10 +11,26 @@
 BF = jnp.bfloat16
 F32 = jnp.float32
 PIECE = 16
+LEAST = 65
 ROWS = 576
 CHUNK = 576
 NT = (((1,), (1,)), ((), ()))
 PARAMS = pltpu.CompilerParams(vmem_limit_bytes=24 * 1024 * 1024)
+
+
+def pieces_of(rows):
+    units = 2 * (rows // PIECE)
+    pairs = max(0, min(units - LEAST, units // 2 - 2))
+    cut = []
+    for which in range(2):
+        first = 0
+        mine = (pairs + 1 - which) // 2
+        while first < rows:
+            size = 2 * PIECE if mine > 0 and first + 2 * PIECE <= rows else PIECE
+            mine -= size > PIECE
+            cut.append((which, first, size))
+            first += size
+    return cut
 
 
 def dot(a, b):
@@ -147,7 +163,6 @@
 
 def up_kernel(lay, rows, chunk, step_ref, x_ref, gate_ref, upper_ref, across_ref, meta_ref, loads_ref, most_ref, *out_refs):
     exp_dev, width, hidden = gate_ref.shape
-    per = rows // PIECE
     me, base = step_ref[0], step_ref[1]
     x = x_ref[...]
     across = across_ref[...]
@@ -197,18 +212,17 @@
         parts = jnp.concatenate(parts, axis=1)
         for which, ref in enumerate((gate_ref, upper_ref)):
             total = dot(parts, ref[...].reshape(exp_dev * width, hidden)).astype(BF)
-            for piece in range(size // PIECE):
-                out_refs[which * per + first // PIECE + piece][...] = total[
-                    piece * PIECE : (piece + 1) * PIECE
-                ]
+            for out_ref, (of, top, tall) in zip(out_refs, pieces_of(rows)):
+                if of == which and first <= top < first + size:
+                    out_ref[...] = total[top - first : top - first + tall]
 
 
 def down_kernel(lay, rows, chunk, adds, step_ref, meta_ref, down_from, table_from, *refs):
     exp_dev, hidden, width = down_from.shape
-    per = rows // PIECE
+    cut = pieces_of(rows)
     refs = list(refs)
     before_ref = refs.pop(0) if adds else None
-    summed, (out_to, held_ref, down_ref, table_ref, out_ref, sems) = refs[: 2 * per], refs[2 * per :]
+    summed, (out_to, held_ref, down_ref, table_ref, out_ref, sems) = refs[: len(cut)], refs[len(cut) :]
     arriving = [
         pltpu.make_async_copy(down_from, down_ref, sems.at[0]),
         pltpu.make_async_copy(table_from, table_ref, sems.at[1]),
@@ -226,9 +240,13 @@
     shift = base.astype(F32)
     for first in range(0, rows, chunk):
         size = min(chunk, rows - first)
-        pieces = range(first // PIECE, (first + size) // PIECE)
-        gate = jnp.concatenate([summed[p][...] for p in pieces], axis=0).astype(F32)
-        upper = jnp.concatenate([summed[per + p][...] for p in pieces], axis=0).astype(F32)
+        gate, upper = (
+            jnp.concatenate(
+                [r[...] for r, (of, top, _) in zip(summed, cut) if of == which and first <= top < first + size],
+                axis=0,
+            ).astype(F32)
+            for which in range(2)
+        )
         inner = (gate / (1.0 + jnp.exp(-gate)) * upper).astype(BF)
         row = (iota((size, width), 0) + first).astype(F32) + shift
         if first == 0:
@@ -262,7 +280,7 @@
 
 def experts(lay, rows, chunk, me, base, before, received, w_gate, w_up, w_down):
     exp_dev, width, hidden = w_gate.shape
-    per = rows // PIECE
+    cut = pieces_of(rows)
     vmem = pl.BlockSpec(memory_space=pltpu.VMEM)
     smem = pl.BlockSpec(memory_space=pltpu.SMEM)
     anywhere = pl.BlockSpec(memory_space=pl.ANY)
@@ -274,9 +292,9 @@
             jax.ShapeDtypeStruct((exp_dev,), jnp.int32),
             jax.ShapeDtypeStruct((1,), jnp.int32),
         ]
-        + [jax.ShapeDtypeStruct((PIECE, hidden), BF)] * (2 * per),
+        + [jax.ShapeDtypeStruct((tall, hidden), BF) for _, _, tall in cut],
         in_specs=[smem] + [vmem] * 4,
-        out_specs=[vmem, smem, smem] + [vmem] * (2 * per),
+        out_specs=[vmem, smem, smem] + [vmem] * len(cut),
         compiler_params=PARAMS,
         name="up",
     )(step, received, w_gate, w_up, jnp.asarray(lay.table.T, BF))
@@ -285,7 +303,7 @@
     out = pl.pallas_call(
         functools.partial(down_kernel, lay, rows, min(chunk, 192), adds),
         out_shape=jax.ShapeDtypeStruct((lay.total, width), BF),
-        in_specs=[smem, vmem, anywhere, anywhere] + [vmem] * (adds + 2 * per),
+        in_specs=[smem, vmem, anywhere, anywhere] + [vmem] * (adds + len(cut)),
         out_specs=anywhere,
         scratch_shapes=[
             pltpu.VMEM((rows, width), BF),

time: 136 us -> 136 us (level)
  no operation moved by 1% of the time
where the time goes in v5:
time: 136 us
  blocking collectives  67.6 us (50%)
  waiting for transfers between devices  28.1 us (21%)
  starting transfers between devices  25.6 us (19%)
  Pallas kernels  12.9 us (9%)
    psum x1, blocking collectives, experts(): summed = lax.psum(parts, 'dp')  67.6 us
    all_to_all x1, starting transfers between devices, body(): lax.all_to_all(expert_out.reshape(columns, lay.rows, width), 'expert', sp...  15 us
    all_to_all x1, waiting for transfers between devices, dispatch(): lax.all_to_all(sending.reshape(lay.columns, lay.rows, width), 'expert', s...  14.3 us
    all_to_all x1, waiting for transfers between devices, body(): lax.all_to_all(expert_out.reshape(columns, lay.rows, width), 'expert', sp...  13.8 us
    all_to_all x1, starting transfers between devices, dispatch(): lax.all_to_all(sending.reshape(lay.columns, lay.rows, width), 'expert', s...  10.6 us
    pallas_call x1, Pallas kernels, experts(): pl.pallas_call(functools.partial(down_kernel, lay, rows, min(chunk, 192),...  4.61 us
    pallas_call x1, Pallas kernels, experts(): pl.pallas_call(functools.partial(up_kernel, lay, rows, chunk), out_shape=...  4.52 us
  transfers between devices with their start and end apart: 2, of which 2 were waited for; matrix products, arithmetic and copies ran while one was open for 0% of the time, Pallas kernels for 0%

profile of v5, /device:TPU:1, one launch (start us, length us, event | category | flops | bytes accessed | tf_op | source)
XLA Modules:
  0.0 135.8 jit_solution(14647689875232360734)
XLA Ops:
  0.6 2.5 %dispatch.2 = bf16[1536,256]{1,0:T(8,128)(2,1)} custom-call(s32[8,56]{1,0:T(8,128)} %bitcast.27, bf16[56,256]{1,0:T(8,128)(2,1)} %tokens_from.1, bf16[1536,128]{1,0:T(8,128)(2,1)} %constant.14.clone.table_from), custom_call_target="tpu_custom_call" | custom-call | tf_op jit(solution)/shard_map/dispatch/pallas_call | solution.py:325
  3.1 0.0 copy-start.33
  3.1 10.6 %all-to-all-start.1 = ((bf16[32,48,256]{2,1,0:T(8,128)(2,1)}), bf16[32,48,256]{2,1,0:T(8,128)(2,1)S(1)}, u32[]{:S(2)}, u32[]{:S(2)}) async-start(bf16[32,48,256]{2,1,0:T(8,128)(2,1)} %bitcast.3), calls=%async_computation.1 | async-start | bytes 1572864 | tf_op jit(solution)/shard_map/all_to_all | solution.py:340
  13.7 0.1 pad_add_fusion.1.step_ref
  13.8 14.3 %all-to-all-done.1 = bf16[32,48,256]{2,1,0:T(8,128)(2,1)S(1)} async-done(((bf16[32,48,256]{2,1,0:T(8,128)(2,1)}), bf16[32,48,256]{2,1,0:T(8,128)(2,1)S(1)}, u32[]{:S(2)}, u32[]{:S(2)}) %all-to-all-start.1) | async-done | bytes 786464 | tf_op jit(solution)/shard_map/all_to_all | solution.py:340
  28.0 0.0 copy-done.33
  28.0 4.5 %up.2 = (f32[8,128]{1,0:T(8,128)S(1)}, s32[2]{0:T(128)}, s32[1]{0:T(128)}, bf16[32,768]{1,0:T(8,128)(2,1)S(1)}, bf16[32,768]{1,0:T(8,128)(2,1)S(1)}, /*index=5*/...) custom-call(s32[2]{0:T(128)S(1)} %pad_add_fusion.1.step_ref, ...), custom_call_target="tpu_custom_call" | custom-call | tf_op jit(solution)/shard_map/up/pallas_call | solution.py:288
  32.6 67.6 %all-reduce.6 = (bf16[32,768]{1,0:T(8,128)(2,1)S(1)}, bf16[32,768]{1,0:T(8,128)(2,1)S(1)}, bf16[32,768]{1,0:T(8,128)(2,1)S(1)}, bf16[32,768]{1,0:T(8,128)(2,1)S(...) all-reduce(bf16[32,768]{1,0:T(8,128)(2,1)S(1)} %get-tuple-element.2, ...), channel_id=1, replica_groups=mesh['dp'=16,'expert'=32] {'dp'}, use_global_device_ids=true, to_apply=%region_0.0 | all-reduce | flops 884736 | bytes 3538944 | tf_op jit(solution)/shard_map/psum | solution.py:301
  100.2 0.0 copy-start.35
  100.2 0.0 copy-start.37
  100.2 4.6 %down.2 = bf16[1536,256]{1,0:T(8,128)(2,1)} custom-call(s32[2]{0:T(128)S(1)} %pad_add_fusion.1.step_ref, f32[8,128]{1,0:T(8,128)S(1)} %get-tuple-element.201.meta_ref, bf16[2,768,256]{2,1,0:T(8,128)(2,1)} %down_from.1, bf16[1536,128]{1,0:T(8,128)(2,1)} %constant.14.clone.table_from, bf16[32,768]{1,0:T(8,128)(2,1)S(1)} %get-tuple-element.618.refs_0_, ...), custom_call_target="tpu_custom_call" | custom-call | tf_op jit(solution)/shard_map/down/pallas_call | solution.py:303
  104.9 0.0 copy-done.35
  104.9 0.0 copy-done.37
  104.9 0.7 while.12
  105.6 0.0 copy-start.32
  105.6 0.0 copy-start.34
  105.6 15.0 %all-to-all-start.2 = ((bf16[32,48,256]{2,1,0:T(8,128)(2,1)}), bf16[32,48,256]{2,1,0:T(8,128)(2,1)S(1)}, u32[]{:S(2)}, u32[]{:S(2)}) async-start(bf16[32,48,256]{2,1,0:T(8,128)(2,1)} %bitcast.6), calls=%async_computation.2 | async-start | bytes 1572864 | tf_op jit(solution)/shard_map/all_to_all | solution.py:373
  120.6 0.0 copy-done.32
  120.6 0.0 copy-done.34
  120.6 0.5 mix.1.matrix_ref
  121.1 13.8 %all-to-all-done.2 = bf16[32,48,256]{2,1,0:T(8,128)(2,1)S(1)} async-done(((bf16[32,48,256]{2,1,0:T(8,128)(2,1)}), bf16[32,48,256]{2,1,0:T(8,128)(2,1)S(1)}, u32[]{:S(2)}, u32[]{:S(2)}) %all-to-all-start.2) | async-done | bytes 786464 | tf_op jit(solution)/shard_map/all_to_all | solution.py:373
  135.0 0.9 combine.1
Async XLA Ops:
  3.1 24.9 %copy-start.33 = (bf16[2,256,768]{2,1,0:T(8,128)(2,1)S(1)}, bf16[2,256,768]{2,1,0:T(8,128)(2,1)}, u32[]{:S(2)}) copy-start(bf16[2,256,768]{2,1,0:T(8,128)(2,1)} %gate_ref.1) | copy-start | bytes 2359300
  3.1 24.9 %all-to-all-start.1 = ((bf16[32,48,256]{2,1,0:T(8,128)(2,1)}), bf16[32,48,256]{2,1,0:T(8,128)(2,1)S(1)}, u32[]{:S(2)}, u32[]{:S(2)}) async-start(bf16[32,48,256]{2,1,0:T(8,128)(2,1)} %bitcast.3), calls=%async_computation.1 | async-start | bytes 1572864 | tf_op jit(solution)/shard_map/all_to_all | solution.py:340
  100.2 4.6 %copy-start.35 = (bf16[56,256]{1,0:T(8,128)(2,1)S(1)}, bf16[56,256]{1,0:T(8,128)(2,1)}, u32[]{:S(2)}) copy-start(bf16[56,256]{1,0:T(8,128)(2,1)} %tokens_from.1) | copy-start | bytes 86020
  100.2 4.6 %copy-start.37 = (s32[56,8]{0,1:T(8,128)S(1)}, s32[56,8]{0,1:T(8,128)}, u32[]{:S(2)}) copy-start(s32[56,8]{0,1:T(8,128)} %param.16) | copy-start | bytes 5380
  105.6 15.0 %copy-start.32 = (f32[56,8]{0,1:T(8,128)S(1)}, f32[56,8]{0,1:T(8,128)}, u32[]{:S(2)}) copy-start(f32[56,8]{0,1:T(8,128)} %param.17) | copy-start | bytes 5380
  105.6 15.0 %copy-start.34 = (bf16[128,1536]{1,0:T(8,128)(2,1)S(1)}, bf16[128,1536]{1,0:T(8,128)(2,1)}, u32[]{:S(2)}) copy-start(bf16[128,1536]{1,0:T(8,128)(2,1)} %get-tuple-element.1056) | copy-start | bytes 1179652
  105.6 29.3 %all-to-all-start.2 = ((bf16[32,48,256]{2,1,0:T(8,128)(2,1)}), bf16[32,48,256]{2,1,0:T(8,128)(2,1)S(1)}, u32[]{:S(2)}, u32[]{:S(2)}) async-start(bf16[32,48,256]{2,1,0:T(8,128)(2,1)} %bitcast.6), calls=%async_computation.2 | async-start | bytes 1572864 | tf_op jit(solution)/shard_map/all_to_all | solution.py:373
